TPU v7x, 32 devices: a whole 2x2x4 slice. The times are simulated.
32 devices in a mesh: seq: 8 (over y, x, core), tp: 4 (over z).
Axes of the slice: x: 2, y: 2, z: 4, core: 2. Of those that a mesh axis runs over, the one named last changes fastest.
Arguments:
- stream: bfloat16 [2048, 1600], P(('seq', 'tp')), may hold values from -6 to 6
- cotangent: bfloat16 [2048, 1600], P(('seq', 'tp')), may hold values from -6 to 6
- segments: int32 [2048], replicated, may hold values from 0 to 4, as said below
- mixer_gain: float32 [1600], replicated, may hold values from 0.5 to 1.5
- query_weight: bfloat16 [1600, 1600], P(None, 'tp'), may hold values from -0.15625 to 0.15625
- key_weight: bfloat16 [1600, 320], P(None, 'tp'), may hold values from -0.15625 to 0.15625
- value_weight: bfloat16 [1600, 320], P(None, 'tp'), may hold values from -0.15625 to 0.15625
- output_weight: bfloat16 [1600, 1600], P(None, 'tp'), may hold values from -0.15625 to 0.15625
- attn_gain: float32 [1600], replicated, may hold values from 0.5 to 1.5
- mamba_gain: float32 [1600], replicated, may hold values from 0.5 to 1.5
- inner_proj: bfloat16 [1600, 3200], P('seq', 'tp'), may hold values from -0.15625 to 0.15625
- inner_gate: bfloat16 [1600, 3200], P('seq', 'tp'), may hold values from -0.15625 to 0.15625
- conv_kernel: float32 [4, 3200], P(None, 'tp'), may hold values from -3 to 3
- conv_bias: float32 [3200], P('tp'), may hold values from -0.5 to 0.5
- select_weight: bfloat16 [3200, 132], P('tp'), may hold values from -0.109375 to 0.109375
- step_weight: float32 [100, 3200], P(None, 'tp'), may hold values from -0.625 to 0.625
- step_bias: float32 [3200], P('tp'), may hold values from -9 to -2
- decay_log: float32 [3200, 16], P('tp'), may hold values from 0 to 2.8
- skip_scale: float32 [3200], P('tp'), may hold values from 0.5 to 1.5
- mamba_out: bfloat16 [1600, 3200], P('seq', 'tp'), may hold values from -0.109375 to 0.109375
- ffn_gain: float32 [1600], replicated, may hold values from 0.5 to 1.5
- ffn_gate: bfloat16 [1600, 5504], P('seq', 'tp'), may hold values from -0.15625 to 0.15625
- ffn_up: bfloat16 [1600, 5504], P('seq', 'tp'), may hold values from -0.15625 to 0.15625
- ffn_down: bfloat16 [1600, 5504], P('seq', 'tp'), may hold values from -0.078125 to 0.078125
Outputs:
- layer_out: bfloat16 [2048, 1600], P(('seq', 'tp'))
- stream_grad: bfloat16 [2048, 1600], P(('seq', 'tp'))
- mixer_gain_grad: float32 [1600], replicated
- query_weight_grad: float32 [1600, 1600], P(None, 'tp')
- key_weight_grad: float32 [1600, 320], P(None, 'tp')
- value_weight_grad: float32 [1600, 320], P(None, 'tp')
- output_weight_grad: float32 [1600, 1600], P(None, 'tp')
- attn_gain_grad: float32 [1600], replicated
- mamba_gain_grad: float32 [1600], replicated
- inner_proj_grad: float32 [1600, 3200], P('seq', 'tp')
- inner_gate_grad: float32 [1600, 3200], P('seq', 'tp')
- conv_kernel_grad: float32 [4, 3200], P(None, 'tp')
- conv_bias_grad: float32 [3200], P('tp')
- select_weight_grad: float32 [3200, 132], P('tp')
- step_weight_grad: float32 [100, 3200], P(None, 'tp')
- step_bias_grad: float32 [3200], P('tp')
- decay_log_grad: float32 [3200, 16], P('tp')
- skip_scale_grad: float32 [3200], P('tp')
- mamba_out_grad: float32 [1600, 3200], P('seq', 'tp')
- ffn_gain_grad: float32 [1600], replicated
- ffn_gate_grad: float32 [1600, 5504], P('seq', 'tp')
- ffn_up_grad: float32 [1600, 5504], P('seq', 'tp')
- ffn_down_grad: float32 [1600, 5504], P('seq', 'tp')
Inputs may be any that keep to these rules, and one draw needn't show every extreme that they name: `segments`: segment numbers start at 0, never fall, and rise by one at each document start. The stream holds five documents. Counting positions from 0, the middle one (number 2) begins at a position from 2 to 128, and its last token is at a position from 1919 to 2045.
All inputs are finite; a program needn't handle non-finite values.
Results may differ from a plain program's by a relative error of at most 0.018.
Values may be sent and summed in bfloat16 or wider, within the bound.
No kernel may reach another device: no remote copies, remote signals or barrier semaphores. Data moves between devices by JAX's collectives and lax.ppermute only.
A program may use at most 256 MiB of HBM per device.

v0:
```python
import jax
import jax.numpy as jnp
from jax import lax
from jax.experimental import pallas as pl
from jax.experimental.pallas import tpu as pltpu
from jax.sharding import PartitionSpec as P
from functools import partial

D = 1600
HEADS = 25
KV_HEADS = 5
HEAD_DIM = 64
STATE = 16
CONV = 4
STEP_RANK = 100
WINDOW = 1024
TOK_DEV = 256
EPS = 1e-06
HIGH = lax.Precision.HIGHEST
NT = (((1,), (1,)), ((), ()))
LANES = 128
HALF = 8
CHUNK = 16
LOG2E = 1.4426950408889634
LN2 = 0.6931471805599453
FAR = 1e6
VMEM_LIMIT = 48 * 1024 * 1024


def lane_groups(width):
    return [(start, min(LANES, width - start)) for start in range(0, width, LANES)]


def tiles(width):
    return [(s, w, n) for s, w in lane_groups(width) for n in range(0, STATE, HALF)]


def spread_row(ref, row):
    return ref[pl.ds(row, 1), :]


def widened(width):
    return -(-width // LANES) * LANES


def end_kernel(reverse, size_in, drive_in, vec_ref, rate_ref, out_ref, size_ref, drive_ref):
    total, width = size_in.shape
    parts = tiles(width)
    size_ref[:, :width] = size_in[...]
    drive_ref[:, :width] = drive_in[...]

    def chunk_step(chunk, held):
        held = list(held)
        at = total // CHUNK - 1 - chunk if reverse else chunk
        for k in range(CHUNK - 1, -1, -1) if reverse else range(CHUNK):
            t = at * CHUNK + k
            sizes = spread_row(size_ref, t)
            drives = spread_row(drive_ref, t)
            for i, (s, w, n) in enumerate(parts):
                size, drive = sizes[:, s : s + w], drives[:, s : s + w]
                factor = jnp.exp2(size * rate_ref[n : n + HALF, s : s + w])
                push = drive * vec_ref[t, n : n + HALF, :w]
                held[i] = factor * (held[i] + push) if reverse else factor * held[i] + push
        return tuple(held)

    held = lax.fori_loop(
        0,
        total // CHUNK,
        chunk_step,
        tuple(jnp.zeros((HALF, w), jnp.float32) for _, w, _ in parts),
    )
    for i, (s, w, n) in enumerate(parts):
        out_ref[n : n + HALF, s : s + w] = held[i]
    out_ref[STATE:, :] = jnp.broadcast_to(
        jnp.sum(size_in[...], 0, keepdims=True), (out_ref.shape[0] - STATE, width)
    )


def entering(reverse, place_ref, ends_ref, rate_ref, into_ref):
    count = ends_ref.shape[0]
    into_ref[...] = jnp.zeros(into_ref.shape, jnp.float32)

    def one(step, carry):
        at = count - 1 - step if reverse else step
        decay = jnp.exp2(rate_ref[...] * ends_ref[at, STATE : STATE + 1, :])
        into_ref[...] = decay * into_ref[...] + ends_ref[at, 0:STATE, :]
        return carry

    lax.fori_loop(0, count - 1 - place_ref[0] if reverse else place_ref[0], one, 0)


def block_mask():
    span = CHUNK * STATE
    row = lax.broadcasted_iota(jnp.int32, (CHUNK, span), 0)
    col = lax.broadcasted_iota(jnp.int32, (CHUNK, span), 1)
    return (col >= row * STATE) & (col < (row + 1) * STATE)


def repeat_matrix():
    span = CHUNK * STATE
    row = lax.broadcasted_iota(jnp.int32, (STATE, span), 0)
    col = lax.broadcasted_iota(jnp.int32, (STATE, span), 1)
    return (lax.rem(col, STATE) == row).astype(jnp.bfloat16)


def picked(vec, mine, repeat):
    wide = jnp.dot(vec.astype(jnp.bfloat16), repeat, preferred_element_type=jnp.float32)
    return jnp.where(mine, wide, 0.0).astype(jnp.bfloat16)


def scan_kernel(
    place_ref, ends_ref, size_in, drive_in, vec_ref, rate_ref, pick_ref,
    y_ref, states_ref, into_ref, size_ref, drive_ref,
):
    total, width = size_in.shape
    parts = tiles(width)
    size_ref[:, :width] = size_in[...]
    drive_ref[:, :width] = drive_in[...]
    entering(False, place_ref, ends_ref, rate_ref, into_ref)
    states_ref[0:STATE, :] = into_ref[...].astype(jnp.bfloat16)
    mine = block_mask()
    repeat = repeat_matrix()

    def chunk_step(chunk, held):
        held = list(held)
        base = chunk * (CHUNK * STATE) + STATE
        for k in range(CHUNK):
            t = chunk * CHUNK + k
            sizes = spread_row(size_ref, t)
            drives = spread_row(drive_ref, t)
            for i, (s, w, n) in enumerate(parts):
                size, drive = sizes[:, s : s + w], drives[:, s : s + w]
                factor = jnp.exp2(size * rate_ref[n : n + HALF, s : s + w])
                held[i] = factor * held[i] + drive * vec_ref[t, n : n + HALF, :w]
                if n == HALF:
                    states_ref[pl.ds(pl.multiple_of(base + k * STATE, STATE), STATE), s : s + w] = (
                        jnp.concatenate([held[i - 1], held[i]], 0).astype(jnp.bfloat16)
                    )
        rows = pl.ds(pl.multiple_of(base, STATE), CHUNK * STATE)
        y_ref[pl.ds(pl.multiple_of(chunk * CHUNK, CHUNK), CHUNK), :] = jnp.dot(
            picked(pick_ref[pl.ds(pl.multiple_of(chunk * CHUNK, CHUNK), CHUNK), :], mine, repeat),
            states_ref[rows, :],
            preferred_element_type=jnp.float32,
        )
        return tuple(held)

    lax.fori_loop(
        0,
        total // CHUNK,
        chunk_step,
        tuple(into_ref[n : n + HALF, s : s + w] for s, w, n in parts),
    )


def back_kernel(
    place_ref, ends_ref, size_in, drive_ref, grad_in, vec_ref, rate_ref, pick_ref, states_ref,
    gdrive_ref, gsize_ref, gentry_ref, gread_ref, grate_ref,
    into_ref, adj_ref, slope_ref, size_ref, grad_ref,
):
    total, width = size_in.shape
    parts = tiles(width)
    size_ref[:, :width] = size_in[...]
    grad_ref[:, :width] = grad_in[...]
    span = CHUNK * STATE
    entering(True, place_ref, ends_ref, rate_ref, into_ref)
    own = block_mask()
    repeat = repeat_matrix()
    mine = own.astype(jnp.float32)
    ones = mine.astype(jnp.bfloat16)
    grate_ref[...] = jnp.zeros(grate_ref.shape, jnp.float32)

    def chunk_step(step, held):
        held = list(held)
        chunk = total // CHUNK - 1 - step
        rates = [jnp.zeros((HALF, w), jnp.float32) for _, w, _ in parts]
        for k in range(CHUNK - 1, -1, -1):
            t = chunk * CHUNK + k
            sizes = spread_row(size_ref, t)
            grads = spread_row(grad_ref, t)
            for i, (s, w, n) in enumerate(parts):
                if n != 0:
                    continue
                size, grad = sizes[:, s : s + w], grads[:, s : s + w]
                before = states_ref[pl.ds(pl.multiple_of(t * STATE, STATE), STATE), s : s + w].astype(
                    jnp.float32
                )
                adjs, slopes = [], []
                for j in range(2):
                    n0 = j * HALF
                    rate = rate_ref[n0 : n0 + HALF, s : s + w]
                    adj = grad * vec_ref[t, n0 : n0 + HALF, :w] + held[i + j]
                    held[i + j] = jnp.exp2(size * rate) * adj
                    moved = held[i + j] * before[n0 : n0 + HALF]
                    rates[i + j] = rates[i + j] + moved * size
                    adjs.append(adj)
                    slopes.append(moved * rate)
                at = slice(k * STATE, (k + 1) * STATE)
                adj_ref[at, s : s + w] = jnp.concatenate(adjs, 0).astype(jnp.bfloat16)
                slope_ref[at, s : s + w] = jnp.concatenate(slopes, 0).astype(jnp.bfloat16)
        for i, (s, w, n) in enumerate(parts):
            grate_ref[n : n + HALF, s : s + w] += rates[i]
        here = pl.ds(pl.multiple_of(chunk * CHUNK, CHUNK), CHUNK)
        gdrive_ref[here, :] = jnp.dot(
            picked(pick_ref[here, :], own, repeat), adj_ref[...], preferred_element_type=jnp.float32
        )
        gsize_ref[here, :] = (
            jnp.dot(ones, slope_ref[...], preferred_element_type=jnp.float32) * LN2
        )
        nt = (((1,), (1,)), ((), ()))
        gentry_ref[pl.ds(chunk, 1), :] = jnp.sum(
            mine
            * lax.dot_general(
                drive_ref[here, :].astype(jnp.bfloat16), adj_ref[...], nt,
                preferred_element_type=jnp.float32,
            ),
            0, keepdims=True,
        )
        rows = pl.ds(pl.multiple_of(chunk * span + STATE, STATE), span)
        gread_ref[pl.ds(chunk, 1), :] = jnp.sum(
            mine
            * lax.dot_general(
                grad_in[here, :].astype(jnp.bfloat16), states_ref[rows, :], nt,
                preferred_element_type=jnp.float32,
            ),
            0, keepdims=True,
        )
        return tuple(held)

    lax.fori_loop(
        0,
        total // CHUNK,
        chunk_step,
        tuple(into_ref[n : n + HALF, s : s + w] for s, w, n in parts),
    )


def cost(total, width, flops, exps, extra):
    cells = total * width * STATE
    return pl.CostEstimate(
        flops=cells * flops, transcendentals=cells * exps, bytes_accessed=total * width * 12 + extra
    )


def rows_scratch(total, width):
    return [pltpu.VMEM((total, widened(width)), jnp.float32)] * 2


def kernel_call(body, outs, scratch, smem, args, estimate):
    vmem = pl.BlockSpec(memory_space=pltpu.VMEM)
    return pl.pallas_call(
        body,
        out_shape=outs,
        in_specs=[pl.BlockSpec(memory_space=pltpu.SMEM)] * smem + [vmem] * (len(args) - smem),
        out_specs=jax.tree.map(lambda _: vmem, outs),
        scratch_shapes=scratch,
        compiler_params=pltpu.CompilerParams(vmem_limit_bytes=VMEM_LIMIT),
        cost_estimate=estimate,
    )(*args)


def block_end(reverse, size, drive, vec, rate):
    total, width = size.shape
    return kernel_call(
        partial(end_kernel, reverse),
        jax.ShapeDtypeStruct((STATE + HALF, width), jnp.float32),
        rows_scratch(total, width), 0, (size, drive, vec, rate),
        cost(total, width, 5, 1, 0),
    )


def scan_forward(place, ends, size, drive, vec, rate, pick):
    total, width = size.shape
    return kernel_call(
        scan_kernel,
        (
            jax.ShapeDtypeStruct((total, width), jnp.float32),
            jax.ShapeDtypeStruct(((total + 1) * STATE, width), jnp.bfloat16),
        ),
        [pltpu.VMEM((STATE, width), jnp.float32)] + rows_scratch(total, width),
        1, (place, ends, size, drive, vec, rate, pick),
        cost(total, width, 6, 1, total * width * 32),
    )


def scan_backward(place, ends, size, drive, grad, vec, rate, pick, states):
    total, width = size.shape
    span = CHUNK * STATE
    return kernel_call(
        back_kernel,
        (
            jax.ShapeDtypeStruct((total, width), jnp.float32),
            jax.ShapeDtypeStruct((total, width), jnp.float32),
            jax.ShapeDtypeStruct((total // CHUNK, span), jnp.float32),
            jax.ShapeDtypeStruct((total // CHUNK, span), jnp.float32),
            jax.ShapeDtypeStruct((STATE, width), jnp.float32),
        ),
        [
            pltpu.VMEM((STATE, width), jnp.float32),
            pltpu.VMEM((span, width), jnp.bfloat16),
            pltpu.VMEM((span, width), jnp.bfloat16),
        ]
        + rows_scratch(total, width),
        1, (place, ends, size, drive, grad, vec, rate, pick, states),
        cost(total, width, 12, 1, total * width * 32),
    )


def lanes_of(vec):
    return jnp.broadcast_to(vec[:, :, None], vec.shape + (LANES,))


def piece_of(head, cols):
    first = lax.div(head * HEAD_DIM, cols)
    last = lax.div(head * HEAD_DIM + HEAD_DIM - 1, cols)
    return first, last, jnp.where(last > first, 1.0, 0.0).astype(jnp.bfloat16)


def pick_head(head, piece, cols, start, width):
    row = lax.broadcasted_iota(jnp.int32, (2 * cols, width), 0)
    lane = lax.broadcasted_iota(jnp.int32, (2 * cols, width), 1)
    source = piece * cols + row
    key = (row < cols) & (lane < HEAD_DIM) & (source == head * HEAD_DIM + lane)
    value = (
        (row >= cols)
        & (lane >= HEAD_DIM)
        & (source - cols == head * HEAD_DIM + lane - HEAD_DIM)
    )
    return (key | value).astype(jnp.bfloat16)


def head_pairs(head, pieces, pair_ref):
    cols = pieces[0].shape[2] // 2
    rows = pieces[0].shape[1]
    first, last, two = piece_of(head, cols)
    pick_first = pick_head(head, first, cols, 0, 2 * HEAD_DIM)
    pick_last = pick_head(head, last, cols, 0, 2 * HEAD_DIM) * two
    for block, ref in enumerate(pieces):
        pair = jnp.dot(ref[first], pick_first, preferred_element_type=jnp.float32) + jnp.dot(
            ref[last], pick_last, preferred_element_type=jnp.float32
        )
        pair_ref[block * rows : (block + 1) * rows, :] = pair.astype(jnp.bfloat16)


def attend_kernel(count, *refs):
    pieces = refs[:count]
    offset_ref, query_seg_ref, key_seg_ref, query_ref, probs_ref, heads_ref = refs[count : count + 6]
    pair_ref, score_ref = refs[count + 6 :]
    head = pl.program_id(0)
    head_pairs(head, pieces, pair_ref)
    quarter = query_seg_ref.shape[0]
    span = key_seg_ref.shape[1]
    row = lax.broadcasted_iota(jnp.int32, (quarter, span), 0)
    col = lax.broadcasted_iota(jnp.int32, (quarter, span), 1)
    distance = row + offset_ref[0] - col
    allowed = (
        (distance >= 0) & (distance < WINDOW) & (query_seg_ref[...] == key_seg_ref[...])
    )
    score_ref[...] = lax.dot_general(
        query_ref[0], pair_ref[:, :HEAD_DIM], NT, preferred_element_type=jnp.float32
    )
    for group in range(query_ref.shape[1] // quarter):
        at = slice(group * quarter, (group + 1) * quarter)
        scores = jnp.where(allowed, score_ref[at, :] * HEAD_DIM ** (-0.5), -1e30)
        raised = jnp.exp(scores - jnp.max(scores, -1, keepdims=True))
        share = 1.0 / jnp.sum(raised, -1, keepdims=True)
        probs_ref[0, at, :] = (raised * share).astype(jnp.bfloat16)
    heads_ref[0] = jnp.dot(
        probs_ref[0], pair_ref[:, HEAD_DIM:], preferred_element_type=jnp.float32
    ).astype(jnp.bfloat16)


def attend_back_kernel(count, *refs):
    pieces = refs[:count]
    query_ref, probs_ref, grad_ref, gquery_ref, gwindow_ref = refs[count : count + 5]
    pair_ref, gprob_ref, gscore_ref = refs[count + 5 :]
    head = pl.program_id(0)
    cols = pieces[0].shape[2] // 2
    first, last, two = piece_of(head, cols)
    head_pairs(head, pieces, pair_ref)
    gprob_ref[...] = lax.dot_general(
        grad_ref[0], pair_ref[:, HEAD_DIM:], NT, preferred_element_type=jnp.float32
    )
    step = HEAD_DIM
    for at in range(0, gprob_ref.shape[0], step):
        probs = probs_ref[0, at : at + step, :].astype(jnp.float32)
        both = probs * gprob_ref[at : at + step, :]
        gscore_ref[at : at + step, :] = (
            both - probs * jnp.sum(both, -1, keepdims=True)
        ).astype(jnp.bfloat16)
    scale = HEAD_DIM ** (-0.5)
    gquery_ref[0] = (
        jnp.dot(gscore_ref[...], pair_ref[:, :HEAD_DIM], preferred_element_type=jnp.float32) * scale
    ).astype(jnp.bfloat16)
    row = lax.broadcasted_iota(jnp.int32, (HEAD_DIM, HEAD_DIM), 0)
    lane = lax.broadcasted_iota(jnp.int32, (HEAD_DIM, HEAD_DIM), 1)
    unit = (row == lane).astype(jnp.bfloat16)

    def turned(value):
        return lax.dot_general(unit, value, NT, preferred_element_type=jnp.float32).astype(
            jnp.bfloat16
        )

    gkey = jnp.dot(turned(query_ref[0]), gscore_ref[...], preferred_element_type=jnp.float32)
    gvalue = jnp.dot(turned(grad_ref[0]), probs_ref[0], preferred_element_type=jnp.float32)
    gpair = jnp.concatenate([gkey * scale, gvalue], 0).astype(jnp.bfloat16)

    @pl.when(head == 0)
    def _():
        gwindow_ref[...] = jnp.zeros(gwindow_ref.shape, jnp.bfloat16)

    def add(piece, weight):
        pick = pick_head(head, piece, cols, 0, 2 * HEAD_DIM) * weight
        part = jnp.dot(pick, gpair, preferred_element_type=jnp.float32)
        gwindow_ref[piece] = (gwindow_ref[piece].astype(jnp.float32) + part).astype(jnp.bfloat16)

    add(first, jnp.ones((), jnp.bfloat16))
    add(last, two)


def whole(shape):
    return pl.BlockSpec(shape, lambda head: (0,) * len(shape))


def of_head(shape):
    return pl.BlockSpec((1,) + shape[1:], lambda head: (head,) + (0,) * (len(shape) - 1))


def attend(pieces, offset, query_seg, key_seg, queries):
    heads, rows, dim = queries.shape
    span = key_seg.shape[1]
    outs = (
        jax.ShapeDtypeStruct((heads, rows, span), jnp.bfloat16),
        jax.ShapeDtypeStruct(queries.shape, jnp.bfloat16),
    )
    return pl.pallas_call(
        partial(attend_kernel, len(pieces)),
        grid=(heads,),
        out_shape=outs,
        in_specs=[whole(p.shape) for p in pieces]
        + [pl.BlockSpec(memory_space=pltpu.SMEM), whole(query_seg.shape), whole(key_seg.shape)]
        + [of_head(queries.shape)],
        out_specs=tuple(of_head(o.shape) for o in outs),
        scratch_shapes=[
            pltpu.VMEM((span, 2 * dim), jnp.bfloat16),
            pltpu.VMEM((rows, span), jnp.float32),
        ],
        compiler_params=pltpu.CompilerParams(vmem_limit_bytes=VMEM_LIMIT),
        cost_estimate=pl.CostEstimate(
            flops=4 * heads * rows * span * dim,
            transcendentals=heads * rows * span,
            bytes_accessed=2 * heads * rows * span + 4 * queries.size,
        ),
    )(*pieces, offset, query_seg, key_seg, queries)


def attend_back(pieces, queries, probs, grads):
    heads, rows, dim = queries.shape
    span = probs.shape[2]
    outs = (
        jax.ShapeDtypeStruct(queries.shape, jnp.bfloat16),
        jax.ShapeDtypeStruct((pieces[0].shape[0], pieces[0].shape[2], span), jnp.bfloat16),
    )
    return pl.pallas_call(
        partial(attend_back_kernel, len(pieces)),
        grid=(heads,),
        out_shape=outs,
        in_specs=[whole(p.shape) for p in pieces]
        + [of_head(queries.shape), of_head(probs.shape), of_head(grads.shape)],
        out_specs=(of_head(outs[0].shape), whole(outs[1].shape)),
        scratch_shapes=[
            pltpu.VMEM((span, 2 * dim), jnp.bfloat16),
            pltpu.VMEM((rows, span), jnp.float32),
            pltpu.VMEM((rows, span), jnp.bfloat16),
        ],
        compiler_params=pltpu.CompilerParams(vmem_limit_bytes=VMEM_LIMIT),
        cost_estimate=pl.CostEstimate(
            flops=8 * heads * rows * span * dim,
            transcendentals=0,
            bytes_accessed=4 * heads * rows * span,
        ),
    )(*pieces, queries, probs, grads)


def passed_along(value, axis, steps):
    count = lax.axis_size(axis)
    first, last = (max(0, -steps), min(count, count - steps))
    return lax.ppermute(value, axis, [(source, source + steps) for source in range(first, last)])


def after(value, *others):
    return lax.optimization_barrier((value, *others))[0]


def partner(value, axis, bit, when=None):
    count = lax.axis_size(axis)
    got = lax.ppermute(value, axis, [(s, s ^ (1 << bit)) for s in range(count)])
    return got if when is None else after(got, when)


def all_sum(value, axes, kind, whens=()):
    whens = list(whens)
    for axis in axes:
        count = lax.axis_size(axis)
        bits = count.bit_length() - 1
        if count != 1 << bits:
            value = lax.psum(value, axis)
            continue
        for bit in range(bits):
            low = value.astype(kind)
            got = partner(low, axis, bit, whens.pop(0) if whens else None)
            value = low.astype(jnp.float32) + got.astype(jnp.float32)
    return value


class Halving:
    def __init__(self, value, order):
        self.order = list(order)
        self.left = sorted(order, reverse=True)
        self.split(value.astype(jnp.bfloat16).reshape([2] * len(self.left) + [-1, value.shape[1]]))

    def split(self, held):
        self.bit = self.order.pop(0)
        axis = self.left.index(self.bit)
        self.left.remove(self.bit)
        mine = (lax.axis_index("seq") >> self.bit) & 1
        self.sent = lax.dynamic_index_in_dim(held, 1 - mine, axis, False)
        self.kept = lax.dynamic_index_in_dim(held, mine, axis, False)

    def step(self, when=None):
        got = partner(self.sent, "seq", self.bit, when)
        total = self.kept.astype(jnp.float32) + got.astype(jnp.float32)
        if self.order:
            self.split(total.astype(jnp.bfloat16))
        return total

    def finish(self, when=None):
        while self.order:
            self.step(when)
        return self.step(when)


def chip_bits():
    return list(range(1, lax.axis_size("seq").bit_length() - 1))


def row_sides(value):
    blocks = lax.axis_size("seq")
    turned = value.T.reshape(blocks // 2, 2, -1, value.shape[0])
    mine = lax.axis_index("seq") & 1
    return [
        lax.dynamic_index_in_dim(turned, side, 1, False).reshape(-1, value.shape[0])
        for side in (mine, 1 - mine)
    ]


def core_send(left_sib, right):
    return matmul(left_sib, right).astype(jnp.bfloat16)


def core_sum(left_own, right, send, when=None):
    got = partner(send, "seq", 0, when)
    return (matmul(left_own, right) + got.astype(jnp.float32)).astype(jnp.bfloat16)


def first_core():
    return (lax.axis_index("seq") & 1) == 0


def core_order(mine, other):
    first = first_core()
    return jnp.where(first, mine, other), jnp.where(first, other, mine)


def chip_groups():
    count = lax.axis_size("seq")
    return [[c for c in range(count) if c % 2 == p] for p in range(2)]


def core_columns(weights, padded_to):
    pad = [(0, 0), (0, padded_to - weights[0].shape[1] // 2)]
    low = jnp.concatenate([jnp.pad(w[:, : w.shape[1] // 2], pad) for w in weights], 1)
    high = jnp.concatenate([jnp.pad(w[:, w.shape[1] // 2 :], pad) for w in weights], 1)
    first = first_core()
    mine, other = jnp.where(first, low, high), jnp.where(first, high, low)
    return jnp.concatenate(core_order(mine, partner(other, "seq", 0)), 0)


def core_rows_back(held, count, width, when):
    mine = lax.axis_index("seq") & 1
    both = held.reshape(2, -1, held.shape[-1])
    kept = lax.dynamic_index_in_dim(both, mine, 0, False)
    sent = lax.dynamic_index_in_dim(both, 1 - mine, 0, False).astype(jnp.bfloat16)
    low, high = core_order(kept, partner(sent, "seq", 0, when).astype(jnp.float32))
    step = held.shape[-1] // count
    return [
        jnp.concatenate([low[:, at : at + width], high[:, at : at + width]], 1)
        for at in range(0, count * step, step)
    ]


def received(pieces, axis):
    count = lax.axis_size(axis)
    place = lax.axis_index(axis)
    held = []
    for shift in range(count):
        sent = lax.dynamic_index_in_dim(pieces, (place + shift) % count, 0, False)
        held.append(
            lax.ppermute(sent, axis, [(s, (s + shift) % count) for s in range(count)])
            if shift
            else sent
        )
    return held


def by_source(held, axis):
    count = lax.axis_size(axis)
    place = lax.axis_index(axis)
    held = jnp.stack(held)
    return jnp.stack(
        [
            lax.dynamic_index_in_dim(held, (place - source) % count, 0, False)
            for source in range(count)
        ]
    )


def exchange(pieces, axis):
    return lax.all_to_all(pieces, axis, 0, 0, tiled=True)


def spread_direct(value, axis, when):
    count = lax.axis_size(axis)
    held = [value]
    for shift in range(1, count):
        got = lax.ppermute(value, axis, [(s, (s + shift) % count) for s in range(count)])
        held.append(after(got, when))
    return by_source(held, axis)


def inverse_rms(value):
    return lax.rsqrt(jnp.mean(value * value, -1, keepdims=True) + EPS)


def rms_back(grad_normed, normed, scale):
    return scale * (grad_normed - normed * jnp.mean(grad_normed * normed, -1, keepdims=True))


def silu_slope(value):
    sigma = jax.nn.sigmoid(value)
    return sigma * (1.0 + value * (1.0 - sigma))


def matmul(left, right):
    return jnp.dot(left, right, preferred_element_type=jnp.float32)


def matmul_nt(left, right):
    return lax.dot_general(
        left, right, (((1,), (1,)), ((), ())), preferred_element_type=jnp.float32
    )


def matmul_tn(left, right):
    return lax.dot_general(
        left, right, (((0,), (0,)), ((), ())), preferred_element_type=jnp.float32
    )


def on_device(
    stream,
    cotangent,
    segments,
    mixer_gain,
    query_weight,
    key_weight,
    value_weight,
    output_weight,
    attn_gain,
    mamba_gain,
    inner_proj,
    inner_gate,
    conv_kernel,
    conv_bias,
    select_weight,
    step_weight,
    step_bias,
    decay_log,
    skip_scale,
    mamba_out,
    ffn_gain,
    ffn_gate,
    ffn_up,
    ffn_down,
):
    seq_count = lax.axis_size("seq")
    tp_count = lax.axis_size("tp")
    seq_index = lax.axis_index("seq")
    tp_index = lax.axis_index("tp")
    quarter = stream.shape[0]
    rows = TOK_DEV
    hops = (WINDOW + TOK_DEV - 1) // TOK_DEV
    span = (hops + 1) * rows
    key_width = KV_HEADS * HEAD_DIM
    groups = HEADS // KV_HEADS
    head_cols = query_weight.shape[1]
    pair_cols = key_weight.shape[1]

    def spread(value):
        return lax.all_gather(value, "tp", axis=0, tiled=True)

    def spread_later(value, when):
        return spread_direct(value, "tp", when).reshape(rows, -1)

    def token_sums(value, when=None):
        pieces = received(value.astype(jnp.bfloat16).reshape(tp_count, quarter, -1), "tp")
        if when is not None:
            pieces = [after(piece, when) for piece in pieces]
        return sum(piece.astype(jnp.float32) for piece in pieces)

    def token_sums_late(value):
        pieces = exchange(value.astype(jnp.bfloat16).reshape(tp_count, quarter, -1), "tp")
        return jnp.sum(pieces.astype(jnp.float32), 0)

    def earlier(value, hop):
        return passed_along(value, "seq", hop)

    def later(value, hop):
        return passed_along(value, "seq", -hop)

    def whole_rows(weight):
        return lax.all_gather(weight, "seq", axis=0, tiled=True)

    def from_chips(value):
        return lax.all_gather(
            value, "seq", axis=0, tiled=True, axis_index_groups=chip_groups()
        )

    def over_chips(value):
        return lax.psum_scatter(
            value, "seq", scatter_dimension=0, tiled=True, axis_index_groups=chip_groups()
        ).astype(jnp.float32)

    def own_cols(value):
        return value.reshape(quarter, tp_count, -1).transpose(1, 0, 2)

    proj = whole_rows(inner_proj)
    wide_cols = -(-inner_gate.shape[1] // LANES) * LANES
    pad_cols = ((0, 0), (0, wide_cols - inner_gate.shape[1]))
    ssm_pair = whole_rows(
        jnp.concatenate([jnp.pad(inner_gate, pad_cols), jnp.pad(mamba_out, pad_cols)], 1)
    )
    zproj = ssm_pair[:, : inner_gate.shape[1]]
    mout = ssm_pair[:, wide_cols : wide_cols + mamba_out.shape[1]]
    block_stream = spread(stream)
    (
        block_stream, stream, cotangent, segments, key_weight, value_weight, conv_kernel,
        conv_bias, decay_log, ffn_gate, ffn_up, ffn_down,
    ) = lax.optimization_barrier(
        (
            block_stream, stream, cotangent, segments, key_weight, value_weight, conv_kernel,
            conv_bias, decay_log, ffn_gate, ffn_up, ffn_down,
        )
    )
    block_stream = block_stream.astype(jnp.float32)
    half = ffn_gate.shape[1] // 2
    wide = -(-half // 256) * 256
    ffn_here = core_columns([ffn_gate, ffn_up, ffn_down], wide)
    ffn_here = ffn_here[:, : 2 * wide], ffn_here[:, 2 * wide :]
    base = seq_index * rows
    first_row = base + tp_index * quarter
    stream_f = stream.astype(jnp.float32)
    scale_one = inverse_rms(stream_f)
    normed_one = stream_f * scale_one
    block_normed = block_stream * inverse_rms(block_stream)
    block_in = (block_normed * mixer_gain).astype(jnp.bfloat16)
    gate_up_w = from_chips(ffn_here[0])
    down_w = from_chips(ffn_here[1])
    pair_weight = jnp.concatenate([key_weight, value_weight], 1)
    query_cols = matmul(block_in, query_weight).astype(jnp.bfloat16)
    pair_part = matmul(block_in, pair_weight).astype(jnp.bfloat16)
    block_late = after(block_in, query_cols, pair_part)
    inner = matmul(block_late, proj).astype(jnp.bfloat16)
    block_pairs = spread_direct(pair_part, "tp", inner)
    edge = earlier(inner[rows - (CONV - 1) :], 1)
    seg_conv = lax.dynamic_slice_in_dim(
        jnp.concatenate([jnp.full((CONV - 1,), -1, jnp.int32), segments]), base, rows + CONV - 1, 0
    )
    own_seg = seg_conv[CONV - 1 :]
    taps = [
        (seg_conv[tap : tap + rows] == own_seg).astype(jnp.float32)[:, None] for tap in range(CONV)
    ]
    padded = jnp.concatenate([edge, inner], 0).astype(jnp.float32)
    conv_pre = conv_bias + sum(
        (conv_kernel[tap] * padded[tap : tap + rows] * taps[tap] for tap in range(CONV))
    )
    alive = (seg_conv[CONV - 2 : CONV - 2 + rows] == own_seg)[:, None]
    mixed_in = jax.nn.silu(conv_pre)
    mixed_low = mixed_in.astype(jnp.bfloat16)
    selected = all_sum(matmul(mixed_low, select_weight), ("tp",), jnp.bfloat16)

    selected = after(selected, block_pairs, *ffn_here)
    step_low = selected[:, :STEP_RANK]
    entry = selected[:, STEP_RANK : STEP_RANK + STATE]
    readout = selected[:, STEP_RANK + STATE :]
    step_pre = jnp.dot(step_low, step_weight, precision=HIGH) + step_bias
    step_size = jax.nn.softplus(step_pre)
    decay = -jnp.exp(decay_log).T
    rate = decay * LOG2E
    size = jnp.where(alive, step_size, FAR)
    drive = step_size * mixed_in
    entry_wide = lanes_of(entry)
    readout_wide = lanes_of(readout)
    ends = block_end(False, size, after(drive, ssm_pair), entry_wide, rate)
    place = seq_index.astype(jnp.int32).reshape(1)
    block_ends = lax.all_gather(ends, "seq")
    scanned, states = scan_forward(
        place, block_ends, size, drive, entry_wide, rate, readout
    )
    zgate_in = matmul(after(block_in, ends), zproj)
    ssm = scanned + skip_scale * mixed_in
    zgate = jax.nn.silu(zgate_in)
    gated = (ssm * zgate).astype(jnp.bfloat16)
    mamba_part = matmul_nt(gated, mout).astype(jnp.bfloat16)
    mamba = token_sums(mamba_part)
    seg_ext = jnp.concatenate([jnp.full((hops * rows,), -1, jnp.int32), segments])
    query_seg = lax.dynamic_slice_in_dim(segments, first_row, quarter, 0)[:, None]
    key_seg = lax.dynamic_slice_in_dim(seg_ext, base, span, 0)[None]
    offset = (hops * rows + tp_index * quarter).astype(jnp.int32).reshape(1)

    def by_head(pieces):
        value = pieces.transpose(1, 0, 2).reshape(quarter, KV_HEADS, groups, HEAD_DIM)
        return value.transpose(1, 2, 0, 3).reshape(KV_HEADS, groups * quarter, HEAD_DIM)

    def by_column(value):
        value = value.reshape(KV_HEADS, groups, quarter, HEAD_DIM).transpose(2, 0, 1, 3)
        return value.reshape(quarter, tp_count, head_cols).transpose(1, 0, 2)

    pieces = [after(earlier(block_pairs, hop), gated) for hop in range(hops, 0, -1)]
    pieces.append(block_pairs)
    queries = by_head(
        after(exchange(query_cols.reshape(tp_count, quarter, head_cols), "tp"), mamba_part)
    )
    probs, heads_out = attend(pieces, offset, query_seg, key_seg, queries)
    heads_cols = exchange(by_column(heads_out), "tp").reshape(rows, head_cols)
    attn_part = matmul_nt(after(heads_cols, mamba), output_weight).astype(jnp.bfloat16)
    mamba = after(mamba, attn_part, gate_up_w)
    attn = token_sums_late(attn_part)

    grad_rows = spread_later(cotangent, mamba)
    scale_attn = inverse_rms(attn)
    normed_attn = attn * scale_attn
    scale_mamba = inverse_rms(mamba)
    normed_mamba = mamba * scale_mamba
    resid = stream_f + 0.5 * (normed_attn * attn_gain + normed_mamba * mamba_gain)
    scale_two = inverse_rms(resid)
    normed_two = resid * scale_two
    ffn_in = (normed_two * ffn_gain).astype(jnp.bfloat16)
    ffn_rows = spread(after(ffn_in, down_w))
    ffn_two = jnp.concatenate([ffn_rows, partner(ffn_rows, "seq", 0)], 0)
    grad_two = jnp.concatenate([grad_rows, partner(grad_rows, "seq", 0, gated)], 0)
    gate_up = matmul(ffn_two, gate_up_w)
    gate, up = gate_up[:, :wide], gate_up[:, wide:]
    activated = (jax.nn.silu(gate) * up).astype(jnp.bfloat16)

    grad_out = cotangent.astype(jnp.float32)
    grad_act_low = matmul(grad_two, down_w).astype(jnp.bfloat16)
    grad_gate = (grad_act_low * up * silu_slope(gate)).astype(jnp.bfloat16)
    grad_up = (grad_act_low * jax.nn.silu(gate)).astype(jnp.bfloat16)
    grad_gate_up = jnp.concatenate([grad_gate, grad_up], 1)

    def chip_tokens(value, weight):
        got = partner(matmul_nt(value[rows:], weight).astype(jnp.bfloat16), "seq", 0)
        return (matmul_nt(value[:rows], weight) + got.astype(jnp.float32)).astype(jnp.bfloat16)

    grad_ffn_part = chip_tokens(grad_gate_up, gate_up_w)
    grad_ffn_in = token_sums(grad_ffn_part)
    gate_up_late, activated_late = lax.optimization_barrier(
        (grad_gate_up, activated, grad_ffn_part)
    )[:2]
    gate_up_grads = matmul_tn(ffn_two, gate_up_late).astype(jnp.bfloat16)
    down_grads = matmul_tn(grad_two, activated_late).astype(jnp.bfloat16)
    bits = chip_bits()
    gate_up_sum = over_chips(gate_up_grads)
    down_x = Halving(down_grads, bits[::-1])
    grad_ffn_in = after(grad_ffn_in, gate_up_grads, down_x.sent)
    grad_ffn_gain = jnp.sum(grad_ffn_in * normed_two, 0)
    grad_resid = grad_out + rms_back(grad_ffn_in * ffn_gain, normed_two, scale_two)
    grad_attn_gain = 0.5 * jnp.sum(grad_resid * normed_attn, 0)
    grad_mamba_gain = 0.5 * jnp.sum(grad_resid * normed_mamba, 0)
    grad_attn = rms_back(0.5 * grad_resid * attn_gain, normed_attn, scale_attn).astype(jnp.bfloat16)
    grad_mamba = rms_back(0.5 * grad_resid * mamba_gain, normed_mamba, scale_mamba).astype(
        jnp.bfloat16
    )
    grad_mrows = spread(grad_mamba)
    grad_arows = exchange(
        jnp.broadcast_to(after(grad_attn, grad_mrows), (tp_count,) + grad_attn.shape), "tp"
    ).reshape(rows, -1)
    grad_gated = matmul(grad_mrows, mout).astype(jnp.bfloat16)
    grad_ssm = grad_gated * zgate
    grad_zgate = (grad_gated * ssm * silu_slope(zgate_in)).astype(jnp.bfloat16)
    grad_skip = jnp.sum(grad_ssm * mixed_in, 0)
    down_x.step(grad_mrows)
    backlog = block_end(True, size, grad_ssm, readout_wide, rate)
    block_backlogs = lax.all_gather(backlog, "seq")

    grad_head_cols = matmul(grad_arows, output_weight).astype(jnp.bfloat16)
    grad_heads = by_head(
        exchange(grad_head_cols.reshape(tp_count, quarter, head_cols), "tp")
    )
    grad_heads = after(grad_heads, down_x.sent)
    mrows_own, mrows_sib = row_sides(after(grad_mrows, grad_ssm))
    block_own, block_sib = row_sides(block_in)
    mout_send = core_send(mrows_sib, gated)
    zgate_send = core_send(block_sib, grad_zgate)
    grad_query, grad_window = attend_back(pieces, queries, probs, grad_heads)
    mout_held = core_sum(mrows_own, gated, mout_send, backlog)
    zgate_held = core_sum(block_own, grad_zgate, zgate_send, backlog)
    window_grad = lax.psum_scatter(after(grad_window, gate_up_sum), "tp", scatter_dimension=0, tiled=False)
    grad_query_cols = exchange(by_column(grad_query), "tp").reshape(rows, head_cols)
    head_grads = jnp.concatenate(
        [matmul_tn(grad_query_cols, block_in), matmul_tn(heads_cols, grad_arows)], 0
    )
    head_grads = head_grads.astype(jnp.bfloat16)
    head_sums = lax.psum(head_grads, "seq")
    mout_x = Halving(mout_held, bits[::-1])
    zgate_x = Halving(zgate_held, bits)
    before_scan = after(
        grad_ssm, mout_x.sent, zgate_x.sent
    )
    grad_drive, grad_size, grad_entry, grad_read, grad_rates = scan_backward(
        place, block_backlogs, size, drive, before_scan, readout_wide, rate, entry, states
    )
    grad_step = grad_size + grad_drive * mixed_in
    grad_inputs = grad_drive * step_size + grad_ssm * skip_scale
    grad_pre = grad_step * jax.nn.sigmoid(step_pre)
    grad_low = jnp.dot(grad_pre, step_weight.T, precision=HIGH)
    grad_low = jnp.concatenate(
        [grad_low, grad_entry.reshape(rows, STATE), grad_read.reshape(rows, STATE)], 1
    )
    grad_decay_log = grad_rates * decay
    grad_step_bias = jnp.sum(grad_pre, 0)
    grad_skip = jnp.sum(grad_ssm * mixed_in, 0)
    grad_step_weight = jnp.dot(step_low.T, grad_pre, precision=HIGH)
    grad_selected = all_sum(grad_low, ("tp",), jnp.bfloat16).astype(jnp.bfloat16)
    moved = [
        later(after(window_grad, grad_low)[:, (hops - hop) * rows : (hops - hop + 1) * rows], hop)
        for hop in range(1, hops + 1)
    ]
    grad_selected = after(grad_selected, window_grad)
    grad_inputs = grad_inputs + matmul_nt(grad_selected, select_weight)
    grad_conv = grad_inputs * silu_slope(conv_pre)
    grad_padded = sum(
        (
            jnp.pad(conv_kernel[tap] * grad_conv * taps[tap], ((tap, CONV - 1 - tap), (0, 0)))
            for tap in range(CONV)
        )
    )
    returned = later(grad_padded[: CONV - 1].astype(jnp.bfloat16), 1).astype(jnp.float32)
    grad_inner = (
        grad_padded[CONV - 1 :] + jnp.pad(returned, ((rows - (CONV - 1), 0), (0, 0)))
    ).astype(jnp.bfloat16)
    down_sum = down_x.finish(grad_selected)
    mout_x.step(grad_selected)
    zgate_x.step(grad_selected)
    layer_sums = token_sums_late(chip_tokens(after(activated, grad_selected), down_w))
    layer_out = (resid + layer_sums).astype(jnp.bfloat16)
    grad_pairs = window_grad[:, hops * rows :].astype(jnp.float32)
    for part in moved:
        grad_pairs = grad_pairs + after(part, grad_conv).astype(jnp.float32)
    grad_pair_low = grad_pairs.astype(jnp.bfloat16)
    pair_grads = matmul(grad_pair_low, block_in)
    grad_inner = after(grad_inner, mout_x.sent, zgate_x.sent, pair_grads)
    proj_send = core_send(block_sib, grad_inner)
    pair_grads = all_sum(pair_grads, ("seq",), jnp.bfloat16, [proj_send] * (len(bits) + 1))
    proj_x = Halving(core_sum(block_own, grad_inner, proj_send), bits[::-1])
    tail = proj_x.sent
    grad_block_rest = (
        matmul_nt(grad_zgate, zproj)
        + matmul_nt(grad_query_cols, query_weight)
        + lax.dot_general(
            grad_pair_low,
            pair_weight,
            (((0,), (1,)), ((), ())),
            preferred_element_type=jnp.float32,
        )
    )
    grad_block_in = matmul_nt(after(grad_inner, proj_send), proj) + grad_block_rest
    block_in_pieces = received(
        grad_block_in.astype(jnp.bfloat16).reshape(tp_count, quarter, -1), "tp"
    )
    proj_sum = proj_x.finish()
    grad_mixer_in = sum(
        after(piece, tail).astype(jnp.float32) for piece in block_in_pieces
    )
    stream_grad = (grad_resid + rms_back(grad_mixer_in * mixer_gain, normed_one, scale_one)).astype(
        jnp.bfloat16
    )
    grad_mixer_gain = jnp.sum(after(grad_block_in, tail) * block_normed, 0)
    gain_parts = jnp.stack([grad_mixer_gain, grad_attn_gain, grad_mamba_gain, grad_ffn_gain])
    gain_parts = all_sum(gain_parts, ("tp",), jnp.float32)
    grad_select = matmul_tn(grad_selected, mixed_low)
    grad_conv_bias = jnp.sum(grad_conv, 0)
    grad_kernel = jnp.stack(
        [jnp.sum(grad_conv * padded[tap : tap + rows] * taps[tap], 0) for tap in range(CONV)]
    )
    width = grad_skip.shape[0]
    gain_rows = -(-gain_parts.size // width)
    gain_flat = jnp.pad(gain_parts.reshape(-1), (0, gain_rows * width - gain_parts.size))
    aligned = [
        gain_flat.reshape(gain_rows, width),
        grad_kernel,
        jnp.stack([grad_conv_bias, grad_step_bias, grad_skip, jnp.zeros_like(grad_skip)]),
        grad_decay_log,
        jnp.pad(grad_select, ((0, -grad_select.shape[0] % HALF), (0, 0))),
        jnp.pad(grad_step_weight, ((0, -STEP_RANK % HALF), (0, 0))),
    ]
    small = jnp.concatenate(aligned, 0).astype(jnp.bfloat16)
    small = all_sum(after(small, tail), ("seq",), jnp.bfloat16)
    mout_sum = mout_x.finish(proj_send)
    zgate_sum = zgate_x.finish(proj_send)
    gate_grad, up_grad = core_rows_back(gate_up_sum, 2, half, proj_send)
    (down_grad,) = core_rows_back(down_sum, 1, half, proj_send)
    head_sums = after(head_sums, proj_sum).astype(jnp.float32)
    ranks = STEP_RANK + 2 * STATE
    starts = [0]
    for part in aligned:
        starts.append(starts[-1] + part.shape[0])
    gain_totals = small[: starts[1]].reshape(-1)[: gain_parts.size].reshape(gain_parts.shape)
    conv_at, lone_at, decay_at, select_at, step_at = starts[1:6]
    return (
        layer_out,
        stream_grad,
        gain_totals[0],
        head_sums[:head_cols].T,
        pair_grads[:pair_cols].T,
        pair_grads[pair_cols:].T,
        head_sums[head_cols:].T,
        gain_totals[1],
        gain_totals[2],
        proj_sum,
        zgate_sum,
        small[conv_at : conv_at + CONV],
        small[lone_at],
        small[select_at : select_at + ranks].T,
        small[step_at : step_at + STEP_RANK],
        small[lone_at + 1],
        small[decay_at : decay_at + STATE].T,
        small[lone_at + 2],
        mout_sum,
        gain_totals[3],
        gate_grad,
        up_grad,
        down_grad,
    )


def solution(mesh):
    return jax.shard_map(
        on_device,
        mesh=mesh,
        in_specs=(
            P(("seq", "tp"), None),
            P(("seq", "tp"), None),
            P(),
            P(),
            P(None, "tp"),
            P(None, "tp"),
            P(None, "tp"),
            P(None, "tp"),
            P(),
            P(),
            P("seq", "tp"),
            P("seq", "tp"),
            P(None, "tp"),
            P("tp"),
            P("tp", None),
            P(None, "tp"),
            P("tp"),
            P("tp", None),
            P("tp"),
            P("seq", "tp"),
            P(),
            P("seq", "tp"),
            P("seq", "tp"),
            P("seq", "tp"),
        ),
        out_specs=(
            P(("seq", "tp"), None),
            P(("seq", "tp"), None),
            P(),
            P(None, "tp"),
            P(None, "tp"),
            P(None, "tp"),
            P(None, "tp"),
            P(),
            P(),
            P("seq", "tp"),
            P("seq", "tp"),
            P(None, "tp"),
            P("tp"),
            P("tp", None),
            P(None, "tp"),
            P("tp"),
            P("tp", None),
            P("tp"),
            P("seq", "tp"),
            P(),
            P("seq", "tp"),
            P("seq", "tp"),
            P("seq", "tp"),
        ),
        check_vma=False,
    )
```

profile of v0, /device:TPU:0, one launch (start us, length us, event | category | flops | bytes accessed | tf_op | source)
XLA Modules:
  0.0 606.3 jit_solution(7855374131267590991)
XLA Ops:
  10.1 22.1 %all_gather.33 = bf16[256,1600]{1,0:T(8,128)(2,1)S(1)} all-gather(bf16[64,1600]{1,0:T(8,128)(2,1)S(1)} %copy-done.53), channel_id=1, replica_groups=mesh['seq'=8,'tp'=4] {'tp'}, dimensions={0}, use_global_device_ids=true | all-gather | bytes 1024000 | tf_op jit(solution)/shard_map/all_gather | solution.py:709
  51.1 4.0 all-to-all-start
  65.3 3.8 collective-permute-start.5
  76.1 6.2 %collective-permute-start.9 = (bf16[4,256,160]{2,1,0:T(8,128)(2,1)S(1)}, bf16[4,256,160]{2,1,0:T(8,128)(2,1)}, u32[]{:S(2)}, u32[]{:S(2)}) collective-permute-start(bf16[4,256,160]{2,1,0:T(8,128)(2,1)S(1)} %pad_maximum_fusion.16.refs_4_), channel_id=1, source_target_pairs={{0,8},{4,12},{8,16},{12,20},{16,24},{20,28},{1,9},{5,13},{9,17},{1... | collective-permute-start | bytes 983048 | tf_op jit(solution)/shard_map/ppermute | solution.py:487
  82.2 4.5 collective-permute-start.8
  97.9 42.1 %all-gather = f32[192,800]{1,0:T(8,128)S(1)} all-gather(f32[24,800]{1,0:T(8,128)S(1)} %shard_map.407), channel_id=2, replica_groups=mesh['seq'=8,'tp'=4] {'seq'}, dimensions={0}, use_global_device_ids=true | all-gather | bytes 691200 | tf_op jit(solution)/shard_map/all_gather | solution.py:815
  140.1 9.9 %shard_map.408 = (f32[256,800]{1,0:T(8,128)S(1)}, bf16[4112,800]{1,0:T(8,128)(2,1)}) custom-call(s32[1]{0:T(128)} %bitcast.4.place_ref, f32[8,24,800]{2,1,0:T(8,128)S(1)} %bitcast.218, f32[256,800]{1,0:T(8,128)S(1)} %copy-done.12, f32[256,800]{1,0:T(8,128)S(1)} %get-tuple-element.117.drive_in.drive_ref, f32[256,16,128]{2,1,0:T(8,128)S(1)} %broadcast_in_dim.24.vec_ref, ...), custom_call_target="tpu_custom_call" | custom-call | flops 19660800 | bytes 9011200 | tf_op jit(solution)/shard_map/pallas_call | solution.py:250
  165.9 11.2 %shard_map.409 = (bf16[5,320,1280]{2,1,0:T(8,128)(2,1)}, bf16[5,320,64]{2,1,0:T(8,128)(2,1)S(1)}) custom-call(bf16[4,256,160]{2,1,0:T(8,128)(2,1)} %collective-permute-done.3.refs_0_, bf16[4,256,160]{2,1,0:T(8,128)(2,1)} %collective-permute-done.8.refs_1_, bf16[4,256,160]{2,1,0:T(8,128)(2,1)} %collective-permute-done.9.refs_2_, ...), custom_call_target="tpu_custom_call" | custom-call | flops 524288000 | bytes 4505600 | tf_op jit(solution)/shard_map/pallas_call | solution.py:435
  178.2 4.9 all-to-all-start.1
  183.1 3.8 collective-permute-start.17
  188.3 11.8 %all-to-all-done.1 = bf16[4,64,400]{2,1,0:T(8,128)(2,1)S(1)} async-done(((bf16[4,64,400]{2,1,0:T(8,128)(2,1)}), bf16[4,64,400]{2,1,0:T(8,128)(2,1)S(1)}, u32[]{:S(2)}, u32[]{:S(2)}) %all-to-all-start.1) | async-done | bytes 204832 | tf_op jit(solution)/shard_map/all_to_all | solution.py:628
  202.2 7.6 %all-to-all-start.2 = ((bf16[4,64,1600]{2,1,0:T(8,128)(2,1)}), bf16[4,64,1600]{2,1,0:T(8,128)(2,1)}, u32[]{:S(2)}, u32[]{:S(2)}) async-start(bf16[4,64,1600]{2,1,0:T(8,128)(2,1)} %bitcast.24), calls=%async_computation.2 | async-start | bytes 1703936 | tf_op jit(solution)/shard_map/all_to_all | solution.py:628
  213.3 17.3 %all-to-all-done.2 = bf16[4,64,1600]{2,1,0:T(8,128)(2,1)} async-done(((bf16[4,64,1600]{2,1,0:T(8,128)(2,1)}), bf16[4,64,1600]{2,1,0:T(8,128)(2,1)}, u32[]{:S(2)}, u32[]{:S(2)}) %all-to-all-start.2) | async-done | bytes 819232 | tf_op jit(solution)/shard_map/all_to_all | solution.py:628
  233.9 19.6 %all_gather.40 = bf16[256,1600]{1,0:T(8,128)(2,1)} all-gather(bf16[64,1600]{1,0:T(8,128)(2,1)S(1)} %multiply_convert_fusion.5), channel_id=1, replica_groups=mesh['seq'=8,'tp'=4] {'tp'}, dimensions={0}, use_global_device_ids=true | all-gather | bytes 1024000 | tf_op jit(solution)/shard_map/all_gather | solution.py:709
  259.5 5.5 fusion.35
  268.1 3.9 convolution_convert_fusion.6
  276.8 4.6 convolution_convert_fusion
  297.6 8.2 %collective-permute-done.21 = bf16[64,1600]{1,0:T(8,128)(2,1)S(1)} collective-permute-done((bf16[64,1600]{1,0:T(8,128)(2,1)S(1)}, bf16[64,1600]{1,0:T(8,128)(2,1)S(1)}, u32[]{:S(2)}, u32[]{:S(2)}) %collective-permute-start.21) | collective-permute-done | bytes 204832 | tf_op jit(solution)/shard_map/ppermute | solution.py:608
  310.4 22.0 %all_gather.41 = bf16[256,1600]{1,0:T(8,128)(2,1)} all-gather(bf16[64,1600]{1,0:T(8,128)(2,1)S(1)} %get-tuple-element.261), channel_id=1, replica_groups=mesh['seq'=8,'tp'=4] {'tp'}, dimensions={0}, use_global_device_ids=true | all-gather | bytes 1024000 | tf_op jit(solution)/shard_map/all_gather | solution.py:709
  333.3 4.4 all-to-all-start.3
  337.7 5.1 multiply_reduce_fusion
  355.7 10.3 %all-gather.1 = f32[192,800]{1,0:T(8,128)} all-gather(f32[24,800]{1,0:T(8,128)S(1)} %shard_map.410), channel_id=3, replica_groups=mesh['seq'=8,'tp'=4] {'seq'}, dimensions={0}, use_global_device_ids=true | all-gather | bytes 691200 | tf_op jit(solution)/shard_map/all_gather | solution.py:904
  373.6 5.1 all-to-all-start.4
  388.3 13.3 %shard_map.412 = (bf16[5,320,64]{2,1,0:T(8,128)(2,1)S(1)}, bf16[4,160,1280]{2,1,0:T(8,128)(2,1)}) custom-call(bf16[4,256,160]{2,1,0:T(8,128)(2,1)} %collective-permute-done.3.refs_0_, bf16[4,256,160]{2,1,0:T(8,128)(2,1)} %collective-permute-done.8.refs_1_, bf16[4,256,160]{2,1,0:T(8,128)(2,1)} %collective-permute-done.9.refs_2_, ...), custom_call_target="tpu_custom_call" | custom-call | flops 1048576000 | bytes 8192000 | tf_op jit(solution)/shard_map/pallas_call | solution.py:463
  412.3 18.9 %shard_map.411 = (f32[256,800]{1,0:T(8,128)S(1)}, f32[256,800]{1,0:T(8,128)S(1)}, f32[16,256]{1,0:T(8,128)S(1)}, f32[16,256]{1,0:T(8,128)S(1)}, f32[16,800]{1,0:T(8,128)S(1)}) custom-call(s32[1]{0:T(128)} %bitcast.4.place_ref, f32[8,24,800]{2,1,0:T(8,128)S(1)} %bitcast.214, f32[256,800]{1,0:T(8,128)S(1)} %copy-done.14, f32[256,800]{1,0:T(8,128)S(1)} %copy-done.11, ...), custom_call_target="tpu_custom_call" | custom-call | flops 39321600 | bytes 9011200 | tf_op jit(solution)/shard_map/pallas_call | solution.py:250
  431.7 3.8 fusion.83
  449.6 6.4 %all-to-all-done.6 = bf16[4,64,400]{2,1,0:T(8,128)(2,1)S(1)} async-done(((bf16[4,64,400]{2,1,0:T(8,128)(2,1)}), bf16[4,64,400]{2,1,0:T(8,128)(2,1)S(1)}, u32[]{:S(2)}, u32[]{:S(2)}) %all-to-all-start.6) | async-done | bytes 204832 | tf_op jit(solution)/shard_map/all_to_all | solution.py:628
  461.0 4.6 convolution_add_fusion
  535.7 4.3 all-to-all-start.5
  554.1 4.6 collective-permute-start.41
  567.1 5.0 collective-permute-done.45
  579.9 7.1 %collective-permute-done.46 = bf16[200,800]{1,0:T(8,128)(2,1)S(1)} collective-permute-done((bf16[200,800]{1,0:T(8,128)(2,1)S(1)}, bf16[200,800]{1,0:T(8,128)(2,1)S(1)}, u32[]{:S(2)}, u32[]{:S(2)}) %collective-permute-start.46) | collective-permute-done | bytes 320032 | tf_op jit(solution)/shard_map/ppermute | solution.py:496
  (641 shorter events, 283.5 us)
Async XLA Ops:
  7.2 50.9 %all-gather.7.cloned.1.call-start = ((), (), s32[]{:S(2)}) async-start(), calls=%async_computation.9 | async-start | bytes 3225600 | tf_op jit(solution)/shard_map/all_gather | solution.py:731
  8.0 85.5 %all-gather.9.cloned.1.call-start = ((), (), s32[]{:S(2)}) async-start(), calls=%async_computation.10 | async-start | bytes 6451200 | tf_op jit(solution)/shard_map/all_gather | solution.py:731
  10.0 199.8 %all-gather.11.cloned.1.call-start = ((), (), s32[]{:S(2)}) async-start(), calls=%async_computation.11 | async-start | bytes 6144000 | tf_op jit(solution)/shard_map/all_gather | solution.py:734
  51.1 112.5 %all-to-all-start = ((bf16[4,64,400]{2,1,0:T(8,128)(2,1)}), bf16[4,64,400]{2,1,0:T(8,128)(2,1)}, u32[]{:S(2)}, u32[]{:S(2)}) async-start(bf16[4,64,400]{2,1,0:T(8,128)(2,1)} %bitcast.9), calls=%async_computation | async-start | bytes 524288 | tf_op jit(solution)/shard_map/all_to_all | solution.py:628
  55.1 178.8 %all-gather.13.cloned.1.call-start = ((), (), s32[]{:S(2)}) async-start(), calls=%async_computation.12 | async-start | bytes 3072000 | tf_op jit(solution)/shard_map/all_gather | solution.py:734
  73.3 85.8 %collective-permute-start.10 = (bf16[4,256,160]{2,1,0:T(8,128)(2,1)S(1)}, bf16[4,256,160]{2,1,0:T(8,128)(2,1)S(1)}, u32[]{:S(2)}, u32[]{:S(2)}) collective-permute-start(bf16[4,256,160]{2,1,0:T(8,128)(2,1)S(1)} %pad_maximum_fusion.16.refs_4_), channel_id=1, source_target_pairs={{0,4},{4,8},{8,12},{12,16},{16,20},{20,24},{24,28},{1,5},{5,9},{9,... | collective-permute-start | bytes 983048 | tf_op jit(solution)/shard_map/ppermute | solution.py:487
  76.1 85.4 %collective-permute-start.9 = (bf16[4,256,160]{2,1,0:T(8,128)(2,1)S(1)}, bf16[4,256,160]{2,1,0:T(8,128)(2,1)}, u32[]{:S(2)}, u32[]{:S(2)}) collective-permute-start(bf16[4,256,160]{2,1,0:T(8,128)(2,1)S(1)} %pad_maximum_fusion.16.refs_4_), channel_id=1, source_target_pairs={{0,8},{4,12},{8,16},{12,20},{16,24},{20,28},{1,9},{5,13},{9,17},{1... | collective-permute-start | bytes 983048 | tf_op jit(solution)/shard_map/ppermute | solution.py:487
  82.2 82.8 %collective-permute-start.8 = (bf16[4,256,160]{2,1,0:T(8,128)(2,1)S(1)}, bf16[4,256,160]{2,1,0:T(8,128)(2,1)}, u32[]{:S(2)}, u32[]{:S(2)}) collective-permute-start(bf16[4,256,160]{2,1,0:T(8,128)(2,1)S(1)} %pad_maximum_fusion.16.refs_4_), channel_id=1, source_target_pairs={{0,12},{4,16},{8,20},{12,24},{16,28},{1,13},{5,17},{9,21},{13,25},... | collective-permute-start | bytes 983048 | tf_op jit(solution)/shard_map/ppermute | solution.py:487
  86.7 78.6 %collective-permute-start.3 = (bf16[4,256,160]{2,1,0:T(8,128)(2,1)S(1)}, bf16[4,256,160]{2,1,0:T(8,128)(2,1)}, u32[]{:S(2)}, u32[]{:S(2)}) collective-permute-start(bf16[4,256,160]{2,1,0:T(8,128)(2,1)S(1)} %pad_maximum_fusion.16.refs_4_), channel_id=1, source_target_pairs={{0,16},{4,20},{8,24},{12,28},{1,17},{5,21},{9,25},{13,29},{2,18},{... | collective-permute-start | bytes 983048 | tf_op jit(solution)/shard_map/ppermute | solution.py:487
  159.1 27.9 %collective-permute-start.12 = (bf16[64,1600]{1,0:T(8,128)(2,1)}, bf16[64,1600]{1,0:T(8,128)(2,1)}, u32[]{:S(2)}, u32[]{:S(2)}) collective-permute-start(bf16[64,1600]{1,0:T(8,128)(2,1)} %get-tuple-element.251), channel_id=1, source_target_pairs={{0,2},{1,3},{2,0},{3,1},{4,6},{5,7},{6,4},{7,5},{8,10},{9,11},{10,... | collective-permute-start | bytes 614408 | tf_op jit(solution)/shard_map/ppermute | solution.py:608
  165.0 44.8 %collective-permute-start.15 = (bf16[64,1600]{1,0:T(8,128)(2,1)}, bf16[64,1600]{1,0:T(8,128)(2,1)}, u32[]{:S(2)}, u32[]{:S(2)}) collective-permute-start(bf16[64,1600]{1,0:T(8,128)(2,1)} %param.25), channel_id=1, source_target_pairs={{0,1},{1,2},{2,3},{3,0},{4,5},{5,6},{6,7},{7,4},{8,9},{9,10},{10,1... | collective-permute-start | bytes 614408 | tf_op jit(solution)/shard_map/ppermute | solution.py:635
  165.4 44.5 %collective-permute-start.16 = (bf16[64,1600]{1,0:T(8,128)(2,1)}, bf16[64,1600]{1,0:T(8,128)(2,1)}, u32[]{:S(2)}, u32[]{:S(2)}) collective-permute-start(bf16[64,1600]{1,0:T(8,128)(2,1)} %param.25), channel_id=1, source_target_pairs={{0,2},{1,3},{2,0},{3,1},{4,6},{5,7},{6,4},{7,5},{8,10},{9,11},{10,... | collective-permute-start | bytes 614408 | tf_op jit(solution)/shard_map/ppermute | solution.py:635
  183.1 26.7 %collective-permute-start.17 = (bf16[64,1600]{1,0:T(8,128)(2,1)}, bf16[64,1600]{1,0:T(8,128)(2,1)S(1)}, u32[]{:S(2)}, u32[]{:S(2)}) collective-permute-start(bf16[64,1600]{1,0:T(8,128)(2,1)} %param.25), channel_id=1, source_target_pairs={{0,3},{1,0},{2,1},{3,2},{4,7},{5,4},{6,5},{7,6},{8,11},{9,8},{10,9... | collective-permute-start | bytes 614408 | tf_op jit(solution)/shard_map/ppermute | solution.py:635
  202.2 28.5 %all-to-all-start.2 = ((bf16[4,64,1600]{2,1,0:T(8,128)(2,1)}), bf16[4,64,1600]{2,1,0:T(8,128)(2,1)}, u32[]{:S(2)}, u32[]{:S(2)}) async-start(bf16[4,64,1600]{2,1,0:T(8,128)(2,1)} %bitcast.24), calls=%async_computation.2 | async-start | bytes 1703936 | tf_op jit(solution)/shard_map/all_to_all | solution.py:628
  209.8 191.8 %reduce-scatter.3.cloned.1.call-start = ((), (), s32[]{:S(2)}) async-start(), calls=%async_computation.13 | async-start | bytes 6144000 | tf_op jit(solution)/shard_map/reduce_scatter | solution.py:739
  212.7 43.0 %collective-permute-start.18 = (bf16[256,1600]{0,1:T(8,128)(2,1)}, bf16[256,1600]{0,1:T(8,128)(2,1)}, u32[]{:S(2)}, u32[]{:S(2)}) collective-permute-start(bf16[256,1600]{0,1:T(8,128)(2,1)} %copy.153), channel_id=1, source_target_pairs={{0,4},{4,0},{8,12},{12,8},{16,20},{20,16},{24,28},{28,24},{1,5},{5... | collective-permute-start | bytes 2457608 | tf_op jit(solution)/shard_map/ppermute | solution.py:496
  295.8 70.2 %collective-permute-start.27 = (bf16[2,400,768]{2,1,0:T(8,128)(2,1)}, bf16[2,400,768]{2,1,0:T(8,128)(2,1)}, u32[]{:S(2)}, u32[]{:S(2)}) collective-permute-start(bf16[2,400,768]{2,1,0:T(8,128)(2,1)} %dynamic-slice_bitcast_fusion), channel_id=1, source_target_pairs={{0,16},{4,20},{8,24},{12,28},{16,0},{20,4},{24,8},{28,12},{1,17},{... | collective-permute-start | bytes 3686408 | tf_op jit(solution)/shard_map/ppermute | solution.py:496
  333.3 37.7 %all-to-all-start.3 = ((bf16[4,64,1600]{2,1,0:T(8,128)(2,1)}), bf16[4,64,1600]{2,1,0:T(8,128)(2,1)}, u32[]{:S(2)}, u32[]{:S(2)}) async-start(bf16[4,64,1600]{2,1,0:T(8,128)(2,1)} %broadcast_in_dim.28), calls=%async_computation.3 | async-start | bytes 1703936 | tf_op jit(solution)/shard_map/all_to_all | solution.py:628
  344.5 37.1 %collective-permute-start.24 = (bf16[800,800]{1,0:T(8,128)(2,1)}, bf16[800,800]{1,0:T(8,128)(2,1)}, u32[]{:S(2)}, u32[]{:S(2)}) collective-permute-start(bf16[800,800]{1,0:T(8,128)(2,1)} %convolution_convert_fusion.8), channel_id=1, source_target_pairs={{0,4},{4,0},{8,12},{12,8},{16,20},{20,16},{24,28},{28,24},{1,5},{5... | collective-permute-start | bytes 3840008 | tf_op jit(solution)/shard_map/ppermute | solution.py:496
  349.5 32.1 %collective-permute-start.23 = (bf16[800,800]{1,0:T(8,128)(2,1)}, bf16[800,800]{1,0:T(8,128)(2,1)}, u32[]{:S(2)}, u32[]{:S(2)}) collective-permute-start(bf16[800,800]{1,0:T(8,128)(2,1)} %convolution_convert_fusion.9), channel_id=1, source_target_pairs={{0,4},{4,0},{8,12},{12,8},{16,20},{20,16},{24,28},{28,24},{1,5},{5... | collective-permute-start | bytes 3840008 | tf_op jit(solution)/shard_map/ppermute | solution.py:496
  369.5 98.3 %collective-permute-start.53 = (bf16[400,768]{1,0:T(8,128)(2,1)}, bf16[400,768]{1,0:T(8,128)(2,1)}, u32[]{:S(2)}, u32[]{:S(2)}) collective-permute-start(bf16[400,768]{1,0:T(8,128)(2,1)} %dynamic-slice_bitcast_fusion.5), channel_id=1, source_target_pairs={{0,8},{4,12},{8,0},{12,4},{16,24},{20,28},{24,16},{28,20},{1,9},{5... | collective-permute-start | bytes 1843208 | tf_op jit(solution)/shard_map/ppermute | solution.py:496
  378.7 89.2 %reduce-scatter.5.cloned.1.call-start = ((), (), s32[]{:S(2)}) async-start(), calls=%async_computation.14 | async-start | bytes 2048000 | tf_op jit(solution)/shard_map/reduce_scatter | solution.py:918
  406.9 62.6 %collective-permute-start.31 = (bf16[2,200,800]{2,1,0:T(8,128)(2,1)}, bf16[2,200,800]{2,1,0:T(8,128)(2,1)}, u32[]{:S(2)}, u32[]{:S(2)}) collective-permute-start(bf16[2,200,800]{2,1,0:T(8,128)(2,1)} %dynamic-slice_bitcast_fusion.2), channel_id=1, source_target_pairs={{0,8},{4,12},{8,0},{12,4},{16,24},{20,28},{24,16},{28,20},{1,9},{5... | collective-permute-start | bytes 1920008 | tf_op jit(solution)/shard_map/ppermute | solution.py:496
  410.9 65.5 %collective-permute-start.30 = (bf16[2,200,800]{2,1,0:T(8,128)(2,1)}, bf16[2,200,800]{2,1,0:T(8,128)(2,1)}, u32[]{:S(2)}, u32[]{:S(2)}) collective-permute-start(bf16[2,200,800]{2,1,0:T(8,128)(2,1)} %dynamic-slice_bitcast_fusion.3), channel_id=1, source_target_pairs={{0,16},{4,20},{8,24},{12,28},{16,0},{20,4},{24,8},{28,12},{1,17},{... | collective-permute-start | bytes 1920008 | tf_op jit(solution)/shard_map/ppermute | solution.py:496
  448.0 139.9 %all-reduce.16.cloned.1.call-start = ((), (), s32[]{:S(2)}) async-start(), calls=%async_computation.15 | async-start | bytes 5324800 | tf_op jit(solution)/shard_map/psum | solution.py:924
  467.8 34.1 %collective-permute-start.52 = (bf16[200,1536]{1,0:T(8,128)(2,1)}, bf16[200,1536]{1,0:T(8,128)(2,1)}, u32[]{:S(2)}, u32[]{:S(2)}) collective-permute-start(bf16[200,1536]{1,0:T(8,128)(2,1)} %fusion.49), channel_id=1, source_target_pairs={{0,4},{4,0},{8,12},{12,8},{16,20},{20,16},{24,28},{28,24},{1,5},{5... | collective-permute-start | bytes 1843208 | tf_op jit(solution)/shard_map/ppermute | solution.py:496
  490.5 26.5 %collective-permute-start.54 = (bf16[200,768]{1,0:T(8,128)(2,1)}, bf16[200,768]{1,0:T(8,128)(2,1)}, u32[]{:S(2)}, u32[]{:S(2)}) collective-permute-start(bf16[200,768]{1,0:T(8,128)(2,1)} %fusion.64), channel_id=1, source_target_pairs={{0,4},{4,0},{8,12},{12,8},{16,20},{20,16},{24,28},{28,24},{1,5},{5... | collective-permute-start | bytes 921608 | tf_op jit(solution)/shard_map/ppermute | solution.py:496
  499.0 29.3 %collective-permute-start.28 = (bf16[256,1600]{0,1:T(8,128)(2,1)}, bf16[256,1600]{0,1:T(8,128)(2,1)}, u32[]{:S(2)}, u32[]{:S(2)}) collective-permute-start(bf16[256,1600]{0,1:T(8,128)(2,1)} %convolution_convert_fusion.3), channel_id=1, source_target_pairs={{0,4},{4,0},{8,12},{12,8},{16,20},{20,16},{24,28},{28,24},{1,5},{5... | collective-permute-start | bytes 2457608 | tf_op jit(solution)/shard_map/ppermute | solution.py:496
  517.1 27.0 %collective-permute-start.36 = (bf16[800,800]{1,0:T(8,128)(2,1)}, bf16[800,800]{1,0:T(8,128)(2,1)}, u32[]{:S(2)}, u32[]{:S(2)}) collective-permute-start(bf16[800,800]{1,0:T(8,128)(2,1)} %convolution_convert_fusion.7), channel_id=1, source_target_pairs={{0,4},{4,0},{8,12},{12,8},{16,20},{20,16},{24,28},{28,24},{1,5},{5... | collective-permute-start | bytes 3840008 | tf_op jit(solution)/shard_map/ppermute | solution.py:496
  519.4 28.8 %collective-permute-start.37 = (bf16[64,1600]{1,0:T(8,128)(2,1)}, bf16[64,1600]{1,0:T(8,128)(2,1)}, u32[]{:S(2)}, u32[]{:S(2)}) collective-permute-start(bf16[64,1600]{1,0:T(8,128)(2,1)} %get-tuple-element.241), channel_id=1, source_target_pairs={{0,1},{1,2},{2,3},{3,0},{4,5},{5,6},{6,7},{7,4},{8,9},{9,10},{10,1... | collective-permute-start | bytes 614408 | tf_op jit(solution)/shard_map/ppermute | solution.py:608
  521.9 27.9 %collective-permute-start.38 = (bf16[64,1600]{1,0:T(8,128)(2,1)}, bf16[64,1600]{1,0:T(8,128)(2,1)}, u32[]{:S(2)}, u32[]{:S(2)}) collective-permute-start(bf16[64,1600]{1,0:T(8,128)(2,1)} %get-tuple-element.240), channel_id=1, source_target_pairs={{0,2},{1,3},{2,0},{3,1},{4,6},{5,7},{6,4},{7,5},{8,10},{9,11},{10,... | collective-permute-start | bytes 614408 | tf_op jit(solution)/shard_map/ppermute | solution.py:608
  535.7 38.5 %all-to-all-start.5 = ((bf16[4,64,1600]{2,1,0:T(8,128)(2,1)}), bf16[4,64,1600]{2,1,0:T(8,128)(2,1)}, u32[]{:S(2)}, u32[]{:S(2)}) async-start(bf16[4,64,1600]{2,1,0:T(8,128)(2,1)} %bitcast.60), calls=%async_computation.7 | async-start | bytes 1703936 | tf_op jit(solution)/shard_map/all_to_all | solution.py:628
  (192 other events, 2133.2 us)
Sparse Core Ops, SparseCore 0:
  9.9 33.8 all-gather.6
  46.3 47.1 all-gather.8
  95.9 80.3 all-gather.10
  178.5 38.2 all-gather.12
  281.5 76.7 reduce-scatter.2
  404.8 34.4 reduce-scatter.4
  461.1 70.0 all-reduce.15
where the time goes:
time: 617 us; the launch traced here: 606 us
  blocking collectives  116 us (19%)
  starting transfers between devices  110 us (18%)
  waiting for transfers between devices  84.2 us (14%)
  matrix products  77.8 us (13%)
  local copies, waits for them, and re-layouts  76.1 us (12%)
  other arithmetic  65.3 us (11%)
  Pallas kernels  59.8 us (10%)
  between operations  16.9 us (3%)
    all_gather x3, blocking collectives, spread(): return lax.all_gather(value, 'tp', axis=0, tiled=True)  63.6 us
    all_gather x1, blocking collectives, on_device(): block_ends = lax.all_gather(ends, 'seq')  42.1 us
    all_to_all x7, waiting for transfers between devices, exchange(): return lax.all_to_all(pieces, axis, 0, 0, tiled=True)  38.7 us
    dot_general x16, matrix products, matmul(): return jnp.dot(left, right, preferred_element_type=jnp.float32)  35.8 us
    pallas_call x4, Pallas kernels, kernel_call(): pl.pallas_call(body, out_shape=outs, in_specs=[pl.BlockSpec(memory_space=...  35.4 us
    all_to_all x7, starting transfers between devices, exchange(): return lax.all_to_all(pieces, axis, 0, 0, tiled=True)  34.1 us
    ppermute x30, waiting for transfers between devices, partner(): got = lax.ppermute(value, axis, [(s, s ^ 1 << bit) for s in range(count)])  31.7 us
    ppermute x30, starting transfers between devices, partner(): got = lax.ppermute(value, axis, [(s, s ^ 1 << bit) for s in range(count)])  29.7 us
  transfers between devices with their start and end apart: 69, of which 21 were waited for; matrix products, arithmetic and copies ran while one was open for 30% of the time, Pallas kernels for 10%

commit v1 on v0

--- a/solution.py
+++ b/solution.py
@@ -2,6 +2,7 @@
 import jax.numpy as jnp
 from jax import lax
 from jax.experimental import pallas as pl
+from jax.experimental.layout import Layout, with_layout_constraint
 from jax.experimental.pallas import tpu as pltpu
 from jax.sharding import PartitionSpec as P
 from functools import partial
@@ -590,10 +591,10 @@
     both = held.reshape(2, -1, held.shape[-1])
     kept = lax.dynamic_index_in_dim(both, mine, 0, False)
     sent = lax.dynamic_index_in_dim(both, 1 - mine, 0, False).astype(jnp.bfloat16)
-    low, high = core_order(kept, partner(sent, "seq", 0, when).astype(jnp.float32))
+    low, high = core_order(kept, partner(sent, "seq", 0, when).astype(kept.dtype))
     step = held.shape[-1] // count
     return [
-        jnp.concatenate([low[:, at : at + width], high[:, at : at + width]], 1)
+        jnp.concatenate([low[:, at : at + width], high[:, at : at + width]], 1).astype(jnp.float32)
         for at in range(0, count * step, step)
     ]
 
@@ -603,7 +604,7 @@
     place = lax.axis_index(axis)
     held = []
     for shift in range(count):
-        sent = lax.dynamic_index_in_dim(pieces, (place + shift) % count, 0, False)
+        sent = row_major(lax.dynamic_index_in_dim(pieces, (place + shift) % count, 0, False))
         held.append(
             lax.ppermute(sent, axis, [(s, (s + shift) % count) for s in range(count)])
             if shift
@@ -630,6 +631,7 @@
 
 def spread_direct(value, axis, when):
     count = lax.axis_size(axis)
+    value = row_major(value)
     held = [value]
     for shift in range(1, count):
         got = lax.ppermute(value, axis, [(s, (s + shift) % count) for s in range(count)])
@@ -658,6 +660,11 @@
     return lax.dot_general(
         left, right, (((1,), (1,)), ((), ())), preferred_element_type=jnp.float32
     )
+
+
+def row_major(value):
+    order = tuple(range(value.ndim))
+    return with_layout_constraint(value, Layout(major_to_minor=order))
 
 
 def matmul_tn(left, right):
@@ -712,7 +719,8 @@
         return spread_direct(value, "tp", when).reshape(rows, -1)
 
     def token_sums(value, when=None):
-        pieces = received(value.astype(jnp.bfloat16).reshape(tp_count, quarter, -1), "tp")
+        value = row_major(value.astype(jnp.bfloat16))
+        pieces = received(value.reshape(tp_count, quarter, -1), "tp")
         if when is not None:
             pieces = [after(piece, when) for piece in pieces]
         return sum(piece.astype(jnp.float32) for piece in pieces)
@@ -738,7 +746,7 @@
     def over_chips(value):
         return lax.psum_scatter(
             value, "seq", scatter_dimension=0, tiled=True, axis_index_groups=chip_groups()
-        ).astype(jnp.float32)
+        )
 
     def own_cols(value):
         return value.reshape(quarter, tp_count, -1).transpose(1, 0, 2)
@@ -762,10 +770,6 @@
         )
     )
     block_stream = block_stream.astype(jnp.float32)
-    half = ffn_gate.shape[1] // 2
-    wide = -(-half // 256) * 256
-    ffn_here = core_columns([ffn_gate, ffn_up, ffn_down], wide)
-    ffn_here = ffn_here[:, : 2 * wide], ffn_here[:, 2 * wide :]
     base = seq_index * rows
     first_row = base + tp_index * quarter
     stream_f = stream.astype(jnp.float32)
@@ -773,13 +777,17 @@
     normed_one = stream_f * scale_one
     block_normed = block_stream * inverse_rms(block_stream)
     block_in = (block_normed * mixer_gain).astype(jnp.bfloat16)
-    gate_up_w = from_chips(ffn_here[0])
-    down_w = from_chips(ffn_here[1])
     pair_weight = jnp.concatenate([key_weight, value_weight], 1)
     query_cols = matmul(block_in, query_weight).astype(jnp.bfloat16)
     pair_part = matmul(block_in, pair_weight).astype(jnp.bfloat16)
     block_late = after(block_in, query_cols, pair_part)
     inner = matmul(block_late, proj).astype(jnp.bfloat16)
+    half = ffn_gate.shape[1] // 2
+    wide = -(-half // 256) * 256
+    ffn_here = core_columns([after(ffn_gate, inner), ffn_up, ffn_down], wide)
+    ffn_here = ffn_here[:, : 2 * wide], ffn_here[:, 2 * wide :]
+    gate_up_w = from_chips(ffn_here[0])
+    down_w = from_chips(ffn_here[1])
     block_pairs = spread_direct(pair_part, "tp", inner)
     edge = earlier(inner[rows - (CONV - 1) :], 1)
     seg_conv = lax.dynamic_slice_in_dim(
@@ -835,16 +843,26 @@
         value = value.reshape(KV_HEADS, groups, quarter, HEAD_DIM).transpose(2, 0, 1, 3)
         return value.reshape(quarter, tp_count, head_cols).transpose(1, 0, 2)
 
-    pieces = [after(earlier(block_pairs, hop), gated) for hop in range(hops, 0, -1)]
+    sent_pairs = after(block_pairs, block_ends)
+    pieces = [after(earlier(sent_pairs, hop), gated) for hop in range(hops, 0, -1)]
     pieces.append(block_pairs)
     queries = by_head(
         after(exchange(query_cols.reshape(tp_count, quarter, head_cols), "tp"), mamba_part)
     )
     probs, heads_out = attend(pieces, offset, query_seg, key_seg, queries)
-    heads_cols = exchange(by_column(heads_out), "tp").reshape(rows, head_cols)
-    attn_part = matmul_nt(after(heads_cols, mamba), output_weight).astype(jnp.bfloat16)
+    heads_held = received(by_column(heads_out), "tp")
+    heads_back = jnp.concatenate(heads_held, 0)
+    attn_part = row_major(
+        matmul_nt(after(heads_back, mamba), output_weight).astype(jnp.bfloat16)
+    )
     mamba = after(mamba, attn_part, gate_up_w)
-    attn = token_sums_late(attn_part)
+    attn = attn_part[:quarter].astype(jnp.float32)
+    for shift in range(1, tp_count):
+        back = [(s, (s - shift) % tp_count) for s in range(tp_count)]
+        part = row_major(attn_part[shift * quarter : (shift + 1) * quarter])
+        attn = attn + lax.ppermute(part, "tp", back).astype(jnp.float32)
+    heads_cols = by_source([after(held, attn_part) for held in heads_held], "tp")
+    heads_cols = heads_cols.reshape(rows, head_cols)
 
     grad_rows = spread_later(cotangent, mamba)
     scale_attn = inverse_rms(attn)
@@ -882,7 +900,8 @@
     bits = chip_bits()
     gate_up_sum = over_chips(gate_up_grads)
     down_x = Halving(down_grads, bits[::-1])
-    grad_ffn_in = after(grad_ffn_in, gate_up_grads, down_x.sent)
+    layer_part = chip_tokens(activated_late, down_w)
+    grad_ffn_in = after(grad_ffn_in, gate_up_grads, down_x.sent, layer_part)
     grad_ffn_gain = jnp.sum(grad_ffn_in * normed_two, 0)
     grad_resid = grad_out + rms_back(grad_ffn_in * ffn_gain, normed_two, scale_two)
     grad_attn_gain = 0.5 * jnp.sum(grad_resid * normed_attn, 0)
@@ -962,7 +981,7 @@
     down_sum = down_x.finish(grad_selected)
     mout_x.step(grad_selected)
     zgate_x.step(grad_selected)
-    layer_sums = token_sums_late(chip_tokens(after(activated, grad_selected), down_w))
+    layer_sums = token_sums(after(layer_part, grad_gated), grad_low)
     layer_out = (resid + layer_sums).astype(jnp.bfloat16)
     grad_pairs = window_grad[:, hops * rows :].astype(jnp.float32)
     for part in moved:
@@ -971,9 +990,9 @@
     pair_grads = matmul(grad_pair_low, block_in)
     grad_inner = after(grad_inner, mout_x.sent, zgate_x.sent, pair_grads)
     proj_send = core_send(block_sib, grad_inner)
-    pair_grads = all_sum(pair_grads, ("seq",), jnp.bfloat16, [proj_send] * (len(bits) + 1))
     proj_x = Halving(core_sum(block_own, grad_inner, proj_send), bits[::-1])
     tail = proj_x.sent
+    pair_grads = all_sum(pair_grads, ("seq",), jnp.bfloat16, [tail] * (len(bits) + 1))
     grad_block_rest = (
         matmul_nt(grad_zgate, zproj)
         + matmul_nt(grad_query_cols, query_weight)
@@ -985,9 +1004,8 @@
         )
     )
     grad_block_in = matmul_nt(after(grad_inner, proj_send), proj) + grad_block_rest
-    block_in_pieces = received(
-        grad_block_in.astype(jnp.bfloat16).reshape(tp_count, quarter, -1), "tp"
-    )
+    block_in_low = row_major(grad_block_in.astype(jnp.bfloat16))
+    block_in_pieces = received(block_in_low.reshape(tp_count, quarter, -1), "tp")
     proj_sum = proj_x.finish()
     grad_mixer_in = sum(
         after(piece, tail).astype(jnp.float32) for piece in block_in_pieces
@@ -1016,10 +1034,10 @@
     ]
     small = jnp.concatenate(aligned, 0).astype(jnp.bfloat16)
     small = all_sum(after(small, tail), ("seq",), jnp.bfloat16)
-    mout_sum = mout_x.finish(proj_send)
-    zgate_sum = zgate_x.finish(proj_send)
-    gate_grad, up_grad = core_rows_back(gate_up_sum, 2, half, proj_send)
-    (down_grad,) = core_rows_back(down_sum, 1, half, proj_send)
+    mout_sum = mout_x.finish(tail)
+    zgate_sum = zgate_x.finish(tail)
+    gate_grad, up_grad = core_rows_back(gate_up_sum, 2, half, tail)
+    (down_grad,) = core_rows_back(down_sum, 1, half, tail)
     head_sums = after(head_sums, proj_sum).astype(jnp.float32)
     ranks = STEP_RANK + 2 * STATE
     starts = [0]

time: 617 us -> 624 us (1.011)
  blocking collectives: 116 us -> 84.1 us
  waiting for transfers between devices: 84.2 us -> 108 us
  starting transfers between devices: 110 us -> 128 us
  other arithmetic: 65.3 us -> 48.6 us
  local copies, waits for them, and re-layouts: 76.1 us -> 85.2 us
  matrix products: 77.8 us -> 85.2 us
    all_to_all x7 -> x4, waiting for transfers between devices: 38.7 us -> 5.37 us  [exchange(): return lax.all_to_all(pieces, axis, 0, 0, tiled=True)]
    all_gather x1, blocking collectives: 42.1 us -> 13.1 us  [on_device(): block_ends = lax.all_gather(ends, 'seq')]
    ppermute x30, starting transfers between devices: 29.7 us -> 55.4 us  [partner(): got = lax.ppermute(value, axis, [(s, s ^ 1 << bit) for s in range(count)])]
    all_to_all x7 -> x4, starting transfers between devices: 34.1 us -> 17 us  [exchange(): return lax.all_to_all(pieces, axis, 0, 0, tiled=True)]
    ppermute x10, waiting for transfers between devices: 2.1 us -> 16 us  [passed_along(): lax.ppermute(value, axis, [(source, source + steps) for source in range(f...]
    ppermute x9 -> x15, waiting for transfers between devices: 9.79 us -> 23 us  [received(): lax.ppermute(sent, axis, [(s, (s + shift) % count) for s in range(count)])]
    ppermute x0 -> x3, waiting for transfers between devices: none -> 10.7 us  [on_device(): attn = attn + lax.ppermute(part, 'tp', back).astype(jnp.float32)]
    unnamed x311 -> x363, local copies, waits for them, and re-layouts: 11.2 us -> 20.8 us
  transfers between devices with their start and end apart: 69 -> 75, of which waited for: 21 -> 27; matrix products, arithmetic and copies ran while one was open for 30% -> 27% of each run, Pallas kernels for 10% -> 9%
where the time goes in v1:
time: 624 us; the launch traced here: 614 us
  starting transfers between devices  128 us (21%)
  waiting for transfers between devices  108 us (17%)
  local copies, waits for them, and re-layouts  85.2 us (14%)
  matrix products  85.2 us (14%)
  blocking collectives  84.1 us (13%)
  Pallas kernels  58.2 us (9%)
  other arithmetic  48.6 us (8%)
  between operations  17.2 us (3%)
    all_gather x3, blocking collectives, spread(): return lax.all_gather(value, 'tp', axis=0, tiled=True)  59.7 us
    ppermute x30, starting transfers between devices, partner(): got = lax.ppermute(value, axis, [(s, s ^ 1 << bit) for s in range(count)])  55.4 us
    dot_general x16, matrix products, matmul(): return jnp.dot(left, right, preferred_element_type=jnp.float32)  35.9 us
    pallas_call x4, Pallas kernels, kernel_call(): pl.pallas_call(body, out_shape=outs, in_specs=[pl.BlockSpec(memory_space=...  35.3 us
    ppermute x30, waiting for transfers between devices, partner(): got = lax.ppermute(value, axis, [(s, s ^ 1 << bit) for s in range(count)])  33.7 us
    dot_general x10, matrix products, matmul_nt(): lax.dot_general(left, right, (((1,), (1,)), ((), ())), preferred_element_...  30 us
    ppermute x15, waiting for transfers between devices, received(): lax.ppermute(sent, axis, [(s, (s + shift) % count) for s in range(count)])  23 us
    unnamed x363, local copies, waits for them, and re-layouts  20.8 us
  transfers between devices with their start and end apart: 75, of which 27 were waited for; matrix products, arithmetic and copies ran while one was open for 27% of the time, Pallas kernels for 9%

profile of v1, /device:TPU:0, one launch (start us, length us, event | category | flops | bytes accessed | tf_op | source)
XLA Modules:
  0.0 614.0 jit_solution(13689516430002188281)
XLA Ops:
  10.2 22.2 %all_gather.33 = bf16[256,1600]{1,0:T(8,128)(2,1)S(1)} all-gather(bf16[64,1600]{1,0:T(8,128)(2,1)S(1)} %copy-done.59), channel_id=1, replica_groups=mesh['seq'=8,'tp'=4] {'tp'}, dimensions={0}, use_global_device_ids=true | all-gather | bytes 1024000 | tf_op jit(solution)/shard_map/all_gather | solution.py:716
  37.2 6.6 %all-gather.7.cloned.1.call-done = bf16[1600,800]{1,0:T(8,128)(2,1)} async-done(((bf16[200,800]{1,0:T(8,128)(2,1)}), bf16[1600,800]{1,0:T(8,128)(2,1)}) %all-gather.7.cloned.1.call-update) | async-done | bytes 2560016 | tf_op jit(solution)/shard_map/all_gather | solution.py:739
  72.3 5.1 collective-permute-start.4
  85.2 6.9 %collective-permute-done.5 = bf16[256,132]{1,0:T(8,128)(2,1)S(1)} collective-permute-done((bf16[256,132]{1,0:T(8,128)(2,1)S(1)}, bf16[256,132]{1,0:T(8,128)(2,1)S(1)}, u32[]{:S(2)}, u32[]{:S(2)}) %collective-permute-start.5) | collective-permute-done | bytes 67616 | tf_op jit(solution)/shard_map/ppermute | solution.py:497
  102.7 13.1 %all-gather = f32[192,800]{1,0:T(8,128)S(1)} all-gather(f32[24,800]{1,0:T(8,128)S(1)} %shard_map.407), channel_id=2, replica_groups=mesh['seq'=8,'tp'=4] {'seq'}, dimensions={0}, use_global_device_ids=true | all-gather | bytes 691200 | tf_op jit(solution)/shard_map/all_gather | solution.py:823
  127.4 9.7 %shard_map.408 = (f32[256,800]{1,0:T(8,128)S(1)}, bf16[4112,800]{1,0:T(8,128)(2,1)}) custom-call(s32[1]{0:T(128)} %bitcast.6.place_ref, f32[8,24,800]{2,1,0:T(8,128)S(1)} %bitcast.228, f32[256,800]{1,0:T(8,128)S(1)} %copy-done.7, f32[256,800]{1,0:T(8,128)S(1)} %get-tuple-element.128.drive_in.drive_ref, f32[256,16,128]{2,1,0:T(8,128)S(1)} %broadcast_in_dim.24.vec_ref, ...), custom_call_target="tpu_custom_call" | custom-call | flops 19660800 | bytes 9011200 | tf_op jit(solution)/shard_map/pallas_call | solution.py:251
  152.5 9.4 %collective-permute-done.8.refs_1_ = bf16[4,256,160]{2,1,0:T(8,128)(2,1)} collective-permute-done((bf16[4,256,160]{2,1,0:T(8,128)(2,1)S(1)}, bf16[4,256,160]{2,1,0:T(8,128)(2,1)}, u32[]{:S(2)}, u32[]{:S(2)}) %collective-permute-start.8) | collective-permute-done | bytes 327712 | tf_op jit(solution)/shard_map/ppermute | solution.py:488
  168.2 11.0 %shard_map.409 = (bf16[5,320,1280]{2,1,0:T(8,128)(2,1)}, bf16[5,320,64]{2,1,0:T(8,128)(2,1)S(1)}) custom-call(bf16[4,256,160]{2,1,0:T(8,128)(2,1)} %collective-permute-done.7.refs_0_, bf16[4,256,160]{2,1,0:T(8,128)(2,1)} %collective-permute-done.8.refs_1_, bf16[4,256,160]{2,1,0:T(8,128)(2,1)S(1)} %copy-done.18, bf16[4,256,160]{2,1,0:T(8,128)(2,1)S(1)} %copy-done.15, ...), custom_call_target="tpu_custom_call" | custom-call | flops 524288000 | bytes 4505600 | tf_op jit(solution)/shard_map/pallas_call | solution.py:436
  198.7 10.7 %collective-permute-done.18 = bf16[64,1600]{1,0:T(8,128)(2,1)S(1)} collective-permute-done((bf16[64,1600]{1,0:T(8,128)(2,1)S(1)}, bf16[64,1600]{1,0:T(8,128)(2,1)S(1)}, u32[]{:S(2)}, u32[]{:S(2)}) %collective-permute-start.18) | collective-permute-done | bytes 204832 | tf_op jit(solution)/shard_map/ppermute | solution.py:863
  218.4 8.2 %all-gather.13.cloned.1.call-done = bf16[1600,768]{1,0:T(8,128)(2,1)} async-done(((bf16[400,768]{1,0:T(8,128)(2,1)}), bf16[1600,768]{1,0:T(8,128)(2,1)}) %all-gather.13.cloned.1.call-update) | async-done | bytes 2457616 | tf_op jit(solution)/shard_map/all_gather | solution.py:742
  226.5 12.3 %collective-permute-start.23 = (bf16[256,1600]{0,1:T(8,128)(2,1)}, bf16[256,1600]{0,1:T(8,128)(2,1)}, u32[]{:S(2)}, u32[]{:S(2)}) collective-permute-start(bf16[256,1600]{0,1:T(8,128)(2,1)} %copy.123), channel_id=1, source_target_pairs={{0,4},{4,0},{8,12},{12,8},{16,20},{20,16},{24,28},{28,24},{1,5},{5... | collective-permute-start | bytes 2457608 | tf_op jit(solution)/shard_map/ppermute | solution.py:497
  238.8 18.9 %all_gather.40 = bf16[256,1600]{1,0:T(8,128)(2,1)S(1)} all-gather(bf16[64,1600]{1,0:T(8,128)(2,1)S(1)} %multiply_convert_fusion.4), channel_id=1, replica_groups=mesh['seq'=8,'tp'=4] {'tp'}, dimensions={0}, use_global_device_ids=true | all-gather | bytes 1024000 | tf_op jit(solution)/shard_map/all_gather | solution.py:716
  263.8 5.3 fusion.33
  269.1 4.3 fusion.20
  273.4 4.4 convolution_convert_fusion.6
  282.6 5.6 add_convert_fusion.3
  288.1 4.6 convolution_convert_fusion
  312.3 9.0 %collective-permute-done.28 = bf16[64,1600]{1,0:T(8,128)(2,1)S(1)} collective-permute-done((bf16[64,1600]{1,0:T(8,128)(2,1)S(1)}, bf16[64,1600]{1,0:T(8,128)(2,1)S(1)}, u32[]{:S(2)}, u32[]{:S(2)}) %collective-permute-start.28) | collective-permute-done | bytes 204832 | tf_op jit(solution)/shard_map/ppermute | solution.py:609
  328.4 18.6 %all_gather.41 = bf16[256,1600]{1,0:T(8,128)(2,1)S(1)} all-gather(bf16[64,1600]{1,0:T(8,128)(2,1)S(1)} %get-tuple-element.290), channel_id=1, replica_groups=mesh['seq'=8,'tp'=4] {'tp'}, dimensions={0}, use_global_device_ids=true | all-gather | bytes 1024000 | tf_op jit(solution)/shard_map/all_gather | solution.py:716
  347.0 4.7 multiply_reduce_fusion
  361.2 4.3 all-to-all-start.1
  371.7 11.3 %all-gather.1 = f32[192,800]{1,0:T(8,128)S(1)} all-gather(f32[24,800]{1,0:T(8,128)S(1)} %shard_map.410), channel_id=3, replica_groups=mesh['seq'=8,'tp'=4] {'seq'}, dimensions={0}, use_global_device_ids=true | all-gather | bytes 691200 | tf_op jit(solution)/shard_map/all_gather | solution.py:923
  398.0 5.1 all-to-all-start.2
  417.7 11.9 %shard_map.412 = (bf16[5,320,64]{2,1,0:T(8,128)(2,1)S(1)}, bf16[4,160,1280]{2,1,0:T(8,128)(2,1)S(1)}) custom-call(bf16[4,256,160]{2,1,0:T(8,128)(2,1)} %collective-permute-done.7.refs_0_, bf16[4,256,160]{2,1,0:T(8,128)(2,1)} %collective-permute-done.8.refs_1_, bf16[4,256,160]{2,1,0:T(8,128)(2,1)S(1)} %copy-done.19, bf16[4,256,160]{2,1,0:T(8,128)(2,1)S(1)} %copy-done.16, ...), custom_call_target="tpu_custom_call" | custom-call | flops 1048576000 | bytes 8192000 | tf_op jit(solution)/shard_map/pallas_call | solution.py:464
  436.3 19.1 %shard_map.411 = (f32[256,800]{1,0:T(8,128)S(1)}, f32[256,800]{1,0:T(8,128)S(1)}, f32[16,256]{1,0:T(8,128)S(1)}, f32[16,256]{1,0:T(8,128)S(1)}, f32[16,800]{1,0:T(8,128)S(1)}) custom-call(s32[1]{0:T(128)} %bitcast.6.place_ref, f32[8,24,800]{2,1,0:T(8,128)S(1)} %bitcast.224, f32[256,800]{1,0:T(8,128)S(1)} %copy-done.9, f32[256,800]{1,0:T(8,128)S(1)} %copy-done.6, ...), custom_call_target="tpu_custom_call" | custom-call | flops 39321600 | bytes 9011200 | tf_op jit(solution)/shard_map/pallas_call | solution.py:251
  477.7 5.2 all-to-all-done.3
  507.8 4.5 collective-permute-start.59
  534.3 4.5 collective-permute-start.54
  538.7 8.7 %collective-permute-done.47 = bf16[64,1600]{1,0:T(8,128)(2,1)S(1)} collective-permute-done((bf16[64,1600]{1,0:T(8,128)(2,1)S(1)}, bf16[64,1600]{1,0:T(8,128)(2,1)S(1)}, u32[]{:S(2)}, u32[]{:S(2)}) %collective-permute-start.47) | collective-permute-done | bytes 204832 | tf_op jit(solution)/shard_map/ppermute | solution.py:609
  560.1 5.8 concatenate.69
  577.8 6.3 %collective-permute-done.52 = bf16[272,800]{1,0:T(8,128)(2,1)S(1)} collective-permute-done((bf16[272,800]{1,0:T(8,128)(2,1)S(1)}, bf16[272,800]{1,0:T(8,128)(2,1)S(1)}, u32[]{:S(2)}, u32[]{:S(2)}) %collective-permute-start.52) | collective-permute-done | bytes 435232 | tf_op jit(solution)/shard_map/ppermute | solution.py:497
  586.0 5.2 collective-permute-done.55
  (706 shorter events, 314.4 us)
Async XLA Ops:
  7.2 36.6 %all-gather.7.cloned.1.call-start = ((), (), s32[]{:S(2)}) async-start(), calls=%async_computation.6 | async-start | bytes 3225600 | tf_op jit(solution)/shard_map/all_gather | solution.py:739
  8.0 89.9 %all-gather.9.cloned.1.call-start = ((), (), s32[]{:S(2)}) async-start(), calls=%async_computation.7 | async-start | bytes 6451200 | tf_op jit(solution)/shard_map/all_gather | solution.py:739
  10.1 199.6 %all-gather.11.cloned.1.call-start = ((), (), s32[]{:S(2)}) async-start(), calls=%async_computation.8 | async-start | bytes 6144000 | tf_op jit(solution)/shard_map/all_gather | solution.py:742
  60.4 90.6 %all-to-all-start = ((bf16[4,64,400]{2,1,0:T(8,128)(2,1)}), bf16[4,64,400]{2,1,0:T(8,128)(2,1)}, u32[]{:S(2)}, u32[]{:S(2)}) async-start(bf16[4,64,400]{2,1,0:T(8,128)(2,1)} %bitcast.9), calls=%async_computation | async-start | bytes 524288 | tf_op jit(solution)/shard_map/all_to_all | solution.py:629
  64.6 162.0 %all-gather.13.cloned.1.call-start = ((), (), s32[]{:S(2)}) async-start(), calls=%async_computation.9 | async-start | bytes 3072000 | tf_op jit(solution)/shard_map/all_gather | solution.py:742
  115.8 29.6 %collective-permute-start.10 = (bf16[4,256,160]{2,1,0:T(8,128)(2,1)S(1)}, bf16[4,256,160]{2,1,0:T(8,128)(2,1)S(1)}, u32[]{:S(2)}, u32[]{:S(2)}) collective-permute-start(bf16[4,256,160]{2,1,0:T(8,128)(2,1)S(1)} %pad_maximum_fusion.14.refs_4_), channel_id=1, source_target_pairs={{0,4},{4,8},{8,12},{12,16},{16,20},{20,24},{24,28},{1,5},{5,9},{9,... | collective-permute-start | bytes 983048 | tf_op jit(solution)/shard_map/ppermute | solution.py:488
  118.1 31.2 %collective-permute-start.9 = (bf16[4,256,160]{2,1,0:T(8,128)(2,1)S(1)}, bf16[4,256,160]{2,1,0:T(8,128)(2,1)S(1)}, u32[]{:S(2)}, u32[]{:S(2)}) collective-permute-start(bf16[4,256,160]{2,1,0:T(8,128)(2,1)S(1)} %pad_maximum_fusion.14.refs_4_), channel_id=1, source_target_pairs={{0,8},{4,12},{8,16},{12,20},{16,24},{20,28},{1,9},{5,13},{9,17},{1... | collective-permute-start | bytes 983048 | tf_op jit(solution)/shard_map/ppermute | solution.py:488
  121.2 40.7 %collective-permute-start.8 = (bf16[4,256,160]{2,1,0:T(8,128)(2,1)S(1)}, bf16[4,256,160]{2,1,0:T(8,128)(2,1)}, u32[]{:S(2)}, u32[]{:S(2)}) collective-permute-start(bf16[4,256,160]{2,1,0:T(8,128)(2,1)S(1)} %pad_maximum_fusion.14.refs_4_), channel_id=1, source_target_pairs={{0,12},{4,16},{8,20},{12,24},{16,28},{1,13},{5,17},{9,21},{13,25},... | collective-permute-start | bytes 983048 | tf_op jit(solution)/shard_map/ppermute | solution.py:488
  125.3 40.8 %collective-permute-start.7 = (bf16[4,256,160]{2,1,0:T(8,128)(2,1)S(1)}, bf16[4,256,160]{2,1,0:T(8,128)(2,1)}, u32[]{:S(2)}, u32[]{:S(2)}) collective-permute-start(bf16[4,256,160]{2,1,0:T(8,128)(2,1)S(1)} %pad_maximum_fusion.14.refs_4_), channel_id=1, source_target_pairs={{0,16},{4,20},{8,24},{12,28},{1,17},{5,21},{9,25},{13,29},{2,18},{... | collective-permute-start | bytes 983048 | tf_op jit(solution)/shard_map/ppermute | solution.py:488
  145.4 36.2 %collective-permute-start.14 = (bf16[64,1600]{1,0:T(8,128)(2,1)}, bf16[64,1600]{1,0:T(8,128)(2,1)}, u32[]{:S(2)}, u32[]{:S(2)}) collective-permute-start(bf16[64,1600]{1,0:T(8,128)(2,1)} %get-tuple-element.274), channel_id=1, source_target_pairs={{0,1},{1,2},{2,3},{3,0},{4,5},{5,6},{6,7},{7,4},{8,9},{9,10},{10,1... | collective-permute-start | bytes 614408 | tf_op jit(solution)/shard_map/ppermute | solution.py:609
  145.4 38.5 %collective-permute-start.16 = (bf16[64,1600]{1,0:T(8,128)(2,1)}, bf16[64,1600]{1,0:T(8,128)(2,1)}, u32[]{:S(2)}, u32[]{:S(2)}) collective-permute-start(bf16[64,1600]{1,0:T(8,128)(2,1)} %get-tuple-element.275), channel_id=1, source_target_pairs={{0,3},{1,0},{2,1},{3,2},{4,7},{5,4},{6,5},{7,6},{8,11},{9,8},{10,9... | collective-permute-start | bytes 614408 | tf_op jit(solution)/shard_map/ppermute | solution.py:609
  150.1 33.9 %collective-permute-start.15 = (bf16[64,1600]{1,0:T(8,128)(2,1)}, bf16[64,1600]{1,0:T(8,128)(2,1)}, u32[]{:S(2)}, u32[]{:S(2)}) collective-permute-start(bf16[64,1600]{1,0:T(8,128)(2,1)} %get-tuple-element.276), channel_id=1, source_target_pairs={{0,2},{1,3},{2,0},{3,1},{4,6},{5,7},{6,4},{7,5},{8,10},{9,11},{10,... | collective-permute-start | bytes 614408 | tf_op jit(solution)/shard_map/ppermute | solution.py:609
  151.0 280.7 %reduce-scatter.3.cloned.1.call-start = ((), (), s32[]{:S(2)}) async-start(), calls=%async_computation.10 | async-start | bytes 6144000 | tf_op jit(solution)/shard_map/reduce_scatter | solution.py:747
  191.5 20.4 %collective-permute-start.21 = (bf16[64,1600]{1,0:T(8,128)(2,1)S(1)}, bf16[64,1600]{1,0:T(8,128)(2,1)}, u32[]{:S(2)}, u32[]{:S(2)}) collective-permute-start(bf16[64,1600]{1,0:T(8,128)(2,1)S(1)} %copy-done.90), channel_id=1, source_target_pairs={{0,2},{1,3},{2,0},{3,1},{4,6},{5,7},{6,4},{7,5},{8,10},{9,11},{10,... | collective-permute-start | bytes 614408 | tf_op jit(solution)/shard_map/ppermute | solution.py:637
  226.5 32.4 %collective-permute-start.23 = (bf16[256,1600]{0,1:T(8,128)(2,1)}, bf16[256,1600]{0,1:T(8,128)(2,1)}, u32[]{:S(2)}, u32[]{:S(2)}) collective-permute-start(bf16[256,1600]{0,1:T(8,128)(2,1)} %copy.123), channel_id=1, source_target_pairs={{0,4},{4,0},{8,12},{12,8},{16,20},{20,16},{24,28},{28,24},{1,5},{5... | collective-permute-start | bytes 2457608 | tf_op jit(solution)/shard_map/ppermute | solution.py:497
  309.5 81.0 %collective-permute-start.37 = (bf16[2,400,768]{2,1,0:T(8,128)(2,1)}, bf16[2,400,768]{2,1,0:T(8,128)(2,1)}, u32[]{:S(2)}, u32[]{:S(2)}) collective-permute-start(bf16[2,400,768]{2,1,0:T(8,128)(2,1)} %dynamic-slice_bitcast_fusion), channel_id=1, source_target_pairs={{0,16},{4,20},{8,24},{12,28},{16,0},{20,4},{24,8},{28,12},{1,17},{... | collective-permute-start | bytes 3686408 | tf_op jit(solution)/shard_map/ppermute | solution.py:497
  356.3 107.7 %collective-permute-start.34 = (bf16[64,1600]{1,0:T(8,128)(2,1)}, bf16[64,1600]{1,0:T(8,128)(2,1)}, u32[]{:S(2)}, u32[]{:S(2)}) collective-permute-start(bf16[64,1600]{1,0:T(8,128)(2,1)} %get-tuple-element.261), channel_id=1, source_target_pairs={{0,3},{1,0},{2,1},{3,2},{4,7},{5,4},{6,5},{7,6},{8,11},{9,8},{10,9... | collective-permute-start | bytes 614408 | tf_op jit(solution)/shard_map/ppermute | solution.py:609
  358.3 103.5 %collective-permute-start.33 = (bf16[64,1600]{1,0:T(8,128)(2,1)}, bf16[64,1600]{1,0:T(8,128)(2,1)}, u32[]{:S(2)}, u32[]{:S(2)}) collective-permute-start(bf16[64,1600]{1,0:T(8,128)(2,1)} %get-tuple-element.262), channel_id=1, source_target_pairs={{0,2},{1,3},{2,0},{3,1},{4,6},{5,7},{6,4},{7,5},{8,10},{9,11},{10,... | collective-permute-start | bytes 614408 | tf_op jit(solution)/shard_map/ppermute | solution.py:609
  358.3 105.3 %collective-permute-start.32 = (bf16[64,1600]{1,0:T(8,128)(2,1)}, bf16[64,1600]{1,0:T(8,128)(2,1)}, u32[]{:S(2)}, u32[]{:S(2)}) collective-permute-start(bf16[64,1600]{1,0:T(8,128)(2,1)} %get-tuple-element.263), channel_id=1, source_target_pairs={{0,1},{1,2},{2,3},{3,0},{4,5},{5,6},{6,7},{7,4},{8,9},{9,10},{10,1... | collective-permute-start | bytes 614408 | tf_op jit(solution)/shard_map/ppermute | solution.py:609
  361.2 34.2 %all-to-all-start.1 = ((bf16[4,64,1600]{2,1,0:T(8,128)(2,1)}), bf16[4,64,1600]{2,1,0:T(8,128)(2,1)}, u32[]{:S(2)}, u32[]{:S(2)}) async-start(bf16[4,64,1600]{2,1,0:T(8,128)(2,1)} %broadcast_in_dim.28), calls=%async_computation.1 | async-start | bytes 1703936 | tf_op jit(solution)/shard_map/all_to_all | solution.py:629
  383.0 23.2 %collective-permute-start.31 = (bf16[800,800]{1,0:T(8,128)(2,1)}, bf16[800,800]{1,0:T(8,128)(2,1)}, u32[]{:S(2)}, u32[]{:S(2)}) collective-permute-start(bf16[800,800]{1,0:T(8,128)(2,1)} %convolution_convert_fusion.8), channel_id=1, source_target_pairs={{0,4},{4,0},{8,12},{12,8},{16,20},{20,16},{24,28},{28,24},{1,5},{5... | collective-permute-start | bytes 3840008 | tf_op jit(solution)/shard_map/ppermute | solution.py:497
  390.5 20.2 %collective-permute-start.30 = (bf16[800,800]{1,0:T(8,128)(2,1)}, bf16[800,800]{1,0:T(8,128)(2,1)}, u32[]{:S(2)}, u32[]{:S(2)}) collective-permute-start(bf16[800,800]{1,0:T(8,128)(2,1)} %convolution_convert_fusion.9), channel_id=1, source_target_pairs={{0,4},{4,0},{8,12},{12,8},{16,20},{20,16},{24,28},{28,24},{1,5},{5... | collective-permute-start | bytes 3840008 | tf_op jit(solution)/shard_map/ppermute | solution.py:497
  403.1 88.1 %reduce-scatter.5.cloned.1.call-start = ((), (), s32[]{:S(2)}) async-start(), calls=%async_computation.11 | async-start | bytes 2048000 | tf_op jit(solution)/shard_map/reduce_scatter | solution.py:937
  406.3 84.9 %collective-permute-start.62 = (bf16[400,768]{1,0:T(8,128)(2,1)}, bf16[400,768]{1,0:T(8,128)(2,1)}, u32[]{:S(2)}, u32[]{:S(2)}) collective-permute-start(bf16[400,768]{1,0:T(8,128)(2,1)} %dynamic-slice_bitcast_fusion.6), channel_id=1, source_target_pairs={{0,8},{4,12},{8,0},{12,4},{16,24},{20,28},{24,16},{28,20},{1,9},{5... | collective-permute-start | bytes 1843208 | tf_op jit(solution)/shard_map/ppermute | solution.py:497
  410.7 80.5 %collective-permute-start.40 = (bf16[2,200,800]{2,1,0:T(8,128)(2,1)}, bf16[2,200,800]{2,1,0:T(8,128)(2,1)}, u32[]{:S(2)}, u32[]{:S(2)}) collective-permute-start(bf16[2,200,800]{2,1,0:T(8,128)(2,1)} %dynamic-slice_bitcast_fusion.2), channel_id=1, source_target_pairs={{0,8},{4,12},{8,0},{12,4},{16,24},{20,28},{24,16},{28,20},{1,9},{5... | collective-permute-start | bytes 1920008 | tf_op jit(solution)/shard_map/ppermute | solution.py:497
  463.7 37.2 %collective-permute-start.39 = (bf16[2,200,800]{2,1,0:T(8,128)(2,1)}, bf16[2,200,800]{2,1,0:T(8,128)(2,1)}, u32[]{:S(2)}, u32[]{:S(2)}) collective-permute-start(bf16[2,200,800]{2,1,0:T(8,128)(2,1)} %dynamic-slice_bitcast_fusion.3), channel_id=1, source_target_pairs={{0,16},{4,20},{8,24},{12,28},{16,0},{20,4},{24,8},{28,12},{1,17},{... | collective-permute-start | bytes 1920008 | tf_op jit(solution)/shard_map/ppermute | solution.py:497
  474.9 117.3 %all-reduce.16.cloned.1.call-start = ((), (), s32[]{:S(2)}) async-start(), calls=%async_computation.12 | async-start | bytes 5324800 | tf_op jit(solution)/shard_map/psum | solution.py:943
  491.2 36.8 %collective-permute-start.61 = (bf16[200,1536]{1,0:T(8,128)(2,1)}, bf16[200,1536]{1,0:T(8,128)(2,1)S(1)}, u32[]{:S(2)}, u32[]{:S(2)}) collective-permute-start(bf16[200,1536]{1,0:T(8,128)(2,1)} %dynamic-slice_bitcast_fusion.5), channel_id=1, source_target_pairs={{0,4},{4,0},{8,12},{12,8},{16,20},{20,16},{24,28},{28,24},{1,5},{5... | collective-permute-start | bytes 1843208 | tf_op jit(solution)/shard_map/ppermute | solution.py:497
  507.8 48.1 %collective-permute-start.59 = (bf16[200,800]{1,0:T(8,128)(2,1)S(1)}, bf16[200,800]{1,0:T(8,128)(2,1)S(1)}, u32[]{:S(2)}, u32[]{:S(2)}) collective-permute-start(bf16[200,800]{1,0:T(8,128)(2,1)S(1)} %dynamic-slice_bitcast_fusion.8), channel_id=1, source_target_pairs={{0,16},{4,20},{8,24},{12,28},{16,0},{20,4},{24,8},{28,12},{1,17},{... | collective-permute-start | bytes 960008 | tf_op jit(solution)/shard_map/ppermute | solution.py:497
  512.3 43.6 %collective-permute-start.60 = (bf16[200,800]{1,0:T(8,128)(2,1)S(1)}, bf16[200,800]{1,0:T(8,128)(2,1)S(1)}, u32[]{:S(2)}, u32[]{:S(2)}) collective-permute-start(bf16[200,800]{1,0:T(8,128)(2,1)S(1)} %dynamic-slice_bitcast_fusion.9), channel_id=1, source_target_pairs={{0,8},{4,12},{8,0},{12,4},{16,24},{20,28},{24,16},{28,20},{1,9},{5... | collective-permute-start | bytes 960008 | tf_op jit(solution)/shard_map/ppermute | solution.py:497
  528.0 19.5 %collective-permute-start.47 = (bf16[64,1600]{1,0:T(8,128)(2,1)S(1)}, bf16[64,1600]{1,0:T(8,128)(2,1)S(1)}, u32[]{:S(2)}, u32[]{:S(2)}) collective-permute-start(bf16[64,1600]{1,0:T(8,128)(2,1)S(1)} %get-tuple-element.258), channel_id=1, source_target_pairs={{0,2},{1,3},{2,0},{3,1},{4,6},{5,7},{6,4},{7,5},{8,10},{9,11},{10,... | collective-permute-start | bytes 614408 | tf_op jit(solution)/shard_map/ppermute | solution.py:609
  534.3 38.6 %collective-permute-start.54 = (bf16[2,200,800]{2,1,0:T(8,128)(2,1)}, bf16[2,200,800]{2,1,0:T(8,128)(2,1)}, u32[]{:S(2)}, u32[]{:S(2)}) collective-permute-start(bf16[2,200,800]{2,1,0:T(8,128)(2,1)} %dynamic-slice_bitcast_fusion.1), channel_id=1, source_target_pairs={{0,16},{4,20},{8,24},{12,28},{16,0},{20,4},{24,8},{28,12},{1,17},{... | collective-permute-start | bytes 1920008 | tf_op jit(solution)/shard_map/ppermute | solution.py:497
  (224 other events, 2131.9 us)
Sparse Core Ops, SparseCore 0:
  9.9 33.8 all-gather.6
  46.3 43.2 all-gather.8
  92.0 94.0 all-gather.10
  188.4 38.1 all-gather.12
  292.9 84.0 reduce-scatter.2
  431.8 37.4 reduce-scatter.4
  486.6 79.3 all-reduce.15

commit v2 on v1

--- a/solution.py
+++ b/solution.py
@@ -785,9 +785,8 @@
     half = ffn_gate.shape[1] // 2
     wide = -(-half // 256) * 256
     ffn_here = core_columns([after(ffn_gate, inner), ffn_up, ffn_down], wide)
-    ffn_here = ffn_here[:, : 2 * wide], ffn_here[:, 2 * wide :]
-    gate_up_w = from_chips(ffn_here[0])
-    down_w = from_chips(ffn_here[1])
+    ffn_w = from_chips(ffn_here)
+    gate_up_w, down_w = ffn_w[:, : 2 * wide], ffn_w[:, 2 * wide :]
     block_pairs = spread_direct(pair_part, "tp", inner)
     edge = earlier(inner[rows - (CONV - 1) :], 1)
     seg_conv = lax.dynamic_slice_in_dim(
@@ -806,11 +805,13 @@
     mixed_low = mixed_in.astype(jnp.bfloat16)
     selected = all_sum(matmul(mixed_low, select_weight), ("tp",), jnp.bfloat16)
 
-    selected = after(selected, block_pairs, *ffn_here)
+    selected = after(selected, block_pairs, ffn_here)
     step_low = selected[:, :STEP_RANK]
     entry = selected[:, STEP_RANK : STEP_RANK + STATE]
     readout = selected[:, STEP_RANK + STATE :]
-    step_pre = jnp.dot(step_low, step_weight, precision=HIGH) + step_bias
+    step_low = step_low.astype(jnp.bfloat16)
+    step_weight_low = step_weight.astype(jnp.bfloat16)
+    step_pre = matmul(step_low, step_weight_low) + step_bias
     step_size = jax.nn.softplus(step_pre)
     decay = -jnp.exp(decay_log).T
     rate = decay * LOG2E
@@ -821,6 +822,9 @@
     ends = block_end(False, size, after(drive, ssm_pair), entry_wide, rate)
     place = seq_index.astype(jnp.int32).reshape(1)
     block_ends = lax.all_gather(ends, "seq")
+    grad_wide = jnp.pad(after(cotangent, selected), ((0, 0), (0, -D % LANES)))
+    grad_wide = spread_later(grad_wide, block_ends)
+    grad_rows = grad_wide[:, :D]
     scanned, states = scan_forward(
         place, block_ends, size, drive, entry_wide, rate, readout
     )
@@ -828,6 +832,7 @@
     ssm = scanned + skip_scale * mixed_in
     zgate = jax.nn.silu(zgate_in)
     gated = (ssm * zgate).astype(jnp.bfloat16)
+    gated = after(gated, grad_wide)
     mamba_part = matmul_nt(gated, mout).astype(jnp.bfloat16)
     mamba = token_sums(mamba_part)
     seg_ext = jnp.concatenate([jnp.full((hops * rows,), -1, jnp.int32), segments])
@@ -847,7 +852,7 @@
     pieces = [after(earlier(sent_pairs, hop), gated) for hop in range(hops, 0, -1)]
     pieces.append(block_pairs)
     queries = by_head(
-        after(exchange(query_cols.reshape(tp_count, quarter, head_cols), "tp"), mamba_part)
+        after(exchange(after(query_cols, ends).reshape(tp_count, quarter, head_cols), "tp"), mamba_part)
     )
     probs, heads_out = attend(pieces, offset, query_seg, key_seg, queries)
     heads_held = received(by_column(heads_out), "tp")
@@ -855,7 +860,7 @@
     attn_part = row_major(
         matmul_nt(after(heads_back, mamba), output_weight).astype(jnp.bfloat16)
     )
-    mamba = after(mamba, attn_part, gate_up_w)
+    mamba = after(mamba, attn_part, ffn_w)
     attn = attn_part[:quarter].astype(jnp.float32)
     for shift in range(1, tp_count):
         back = [(s, (s - shift) % tp_count) for s in range(tp_count)]
@@ -864,7 +869,6 @@
     heads_cols = by_source([after(held, attn_part) for held in heads_held], "tp")
     heads_cols = heads_cols.reshape(rows, head_cols)
 
-    grad_rows = spread_later(cotangent, mamba)
     scale_attn = inverse_rms(attn)
     normed_attn = attn * scale_attn
     scale_mamba = inverse_rms(mamba)
@@ -873,9 +877,12 @@
     scale_two = inverse_rms(resid)
     normed_two = resid * scale_two
     ffn_in = (normed_two * ffn_gain).astype(jnp.bfloat16)
-    ffn_rows = spread(after(ffn_in, down_w))
-    ffn_two = jnp.concatenate([ffn_rows, partner(ffn_rows, "seq", 0)], 0)
-    grad_two = jnp.concatenate([grad_rows, partner(grad_rows, "seq", 0, gated)], 0)
+    grad_other = partner(grad_wide, "seq", 0, mamba)
+    grad_two = jnp.concatenate([grad_wide, grad_other], 0)[:, :D]
+    ffn_wide = jnp.pad(after(ffn_in, grad_other), ((0, 0), (0, -D % LANES)))
+    ffn_rows = spread(ffn_wide)
+    ffn_other = partner(ffn_rows, "seq", 0)
+    ffn_two = jnp.concatenate([ffn_rows, ffn_other], 0)[:, :D]
     gate_up = matmul(ffn_two, gate_up_w)
     gate, up = gate_up[:, :wide], gate_up[:, wide:]
     activated = (jax.nn.silu(gate) * up).astype(jnp.bfloat16)
@@ -887,7 +894,8 @@
     grad_gate_up = jnp.concatenate([grad_gate, grad_up], 1)
 
     def chip_tokens(value, weight):
-        got = partner(matmul_nt(value[rows:], weight).astype(jnp.bfloat16), "seq", 0)
+        sent = matmul_nt(value[rows:], weight).astype(jnp.bfloat16)
+        got = partner(jnp.pad(sent, ((0, 0), (0, -D % LANES))), "seq", 0)[:, :D]
         return (matmul_nt(value[:rows], weight) + got.astype(jnp.float32)).astype(jnp.bfloat16)
 
     grad_ffn_part = chip_tokens(grad_gate_up, gate_up_w)
@@ -952,14 +960,15 @@
     grad_step = grad_size + grad_drive * mixed_in
     grad_inputs = grad_drive * step_size + grad_ssm * skip_scale
     grad_pre = grad_step * jax.nn.sigmoid(step_pre)
-    grad_low = jnp.dot(grad_pre, step_weight.T, precision=HIGH)
+    grad_pre_low = grad_pre.astype(jnp.bfloat16)
+    grad_low = matmul_nt(grad_pre_low, step_weight_low)
     grad_low = jnp.concatenate(
         [grad_low, grad_entry.reshape(rows, STATE), grad_read.reshape(rows, STATE)], 1
     )
     grad_decay_log = grad_rates * decay
     grad_step_bias = jnp.sum(grad_pre, 0)
     grad_skip = jnp.sum(grad_ssm * mixed_in, 0)
-    grad_step_weight = jnp.dot(step_low.T, grad_pre, precision=HIGH)
+    grad_step_weight = matmul_tn(step_low, grad_pre_low)
     grad_selected = all_sum(grad_low, ("tp",), jnp.bfloat16).astype(jnp.bfloat16)
     moved = [
         later(after(window_grad, grad_low)[:, (hops - hop) * rows : (hops - hop + 1) * rows], hop)
@@ -1018,41 +1027,47 @@
     gain_parts = all_sum(gain_parts, ("tp",), jnp.float32)
     grad_select = matmul_tn(grad_selected, mixed_low)
     grad_conv_bias = jnp.sum(grad_conv, 0)
-    grad_kernel = jnp.stack(
-        [jnp.sum(grad_conv * padded[tap : tap + rows] * taps[tap], 0) for tap in range(CONV)]
-    )
+    lone_rows = [
+        jnp.sum(grad_conv * padded[tap : tap + rows] * taps[tap], 0) for tap in range(CONV)
+    ] + [grad_conv_bias, grad_step_bias, grad_skip, jnp.zeros_like(grad_skip)]
     width = grad_skip.shape[0]
     gain_rows = -(-gain_parts.size // width)
     gain_flat = jnp.pad(gain_parts.reshape(-1), (0, gain_rows * width - gain_parts.size))
     aligned = [
         gain_flat.reshape(gain_rows, width),
-        grad_kernel,
-        jnp.stack([grad_conv_bias, grad_step_bias, grad_skip, jnp.zeros_like(grad_skip)]),
+        jnp.stack(lone_rows),
         grad_decay_log,
         jnp.pad(grad_select, ((0, -grad_select.shape[0] % HALF), (0, 0))),
         jnp.pad(grad_step_weight, ((0, -STEP_RANK % HALF), (0, 0))),
     ]
-    small = jnp.concatenate(aligned, 0).astype(jnp.bfloat16)
+    height = sum(part.shape[0] for part in aligned)
+    small, above = 0.0, 0
+    for part in aligned:
+        below = height - above - part.shape[0]
+        small = small + jnp.pad(part.astype(jnp.float32), ((above, below), (0, 0)))
+        above += part.shape[0]
+    small = small.astype(jnp.bfloat16)
     small = all_sum(after(small, tail), ("seq",), jnp.bfloat16)
     mout_sum = mout_x.finish(tail)
     zgate_sum = zgate_x.finish(tail)
     gate_grad, up_grad = core_rows_back(gate_up_sum, 2, half, tail)
     (down_grad,) = core_rows_back(down_sum, 1, half, tail)
-    head_sums = after(head_sums, proj_sum).astype(jnp.float32)
+    head_sums = after(head_sums, proj_sum)
     ranks = STEP_RANK + 2 * STATE
     starts = [0]
     for part in aligned:
         starts.append(starts[-1] + part.shape[0])
     gain_totals = small[: starts[1]].reshape(-1)[: gain_parts.size].reshape(gain_parts.shape)
-    conv_at, lone_at, decay_at, select_at, step_at = starts[1:6]
+    conv_at, decay_at, select_at, step_at = starts[1:5]
+    lone_at = conv_at + CONV
     return (
         layer_out,
         stream_grad,
         gain_totals[0],
-        head_sums[:head_cols].T,
+        head_sums[:head_cols].T.astype(jnp.float32),
         pair_grads[:pair_cols].T,
         pair_grads[pair_cols:].T,
-        head_sums[head_cols:].T,
+        head_sums[head_cols:].T.astype(jnp.float32),
         gain_totals[1],
         gain_totals[2],
         proj_sum,

time: 624 us -> 605 us (0.970)
  local copies, waits for them, and re-layouts: 85.2 us -> 70.1 us
  waiting for transfers between devices: 108 us -> 93.9 us
  other arithmetic: 48.6 us -> 58.9 us
    ppermute x10, waiting for transfers between devices: 16 us -> 7.4 us  [passed_along(): lax.ppermute(value, axis, [(source, source + steps) for source in range(f...]
    all_gather x2 -> x1, waiting for transfers between devices: 8.18 us -> 0.02 us  [from_chips(): lax.all_gather(value, 'seq', axis=0, tiled=True, axis_index_groups=chip_g...]
    ppermute x3 -> x0, local copies, waits for them, and re-layouts: 6.55 us -> none  [partner(): got = lax.ppermute(value, axis, [(s, s ^ 1 << bit) for s in range(count)])]
    dot_general x3 -> x0, matrix products: 6.33 us -> none  [the longest x1 4.03 us: on_device(): step_pre = jnp.dot(step_low, step_weight, precision=HIGH) + step_bias]
    dot_general x5 -> x6, matrix products: 12.5 us -> 16.3 us  [matmul_tn(): lax.dot_general(left, right, (((0,), (0,)), ((), ())), preferred_element_...]
    dot_general x10 -> x11, matrix products: 30 us -> 27.7 us  [matmul_nt(): lax.dot_general(left, right, (((1,), (1,)), ((), ())), preferred_element_...]
    dot_general x16 -> x17, matrix products: 35.9 us -> 38 us  [matmul(): return jnp.dot(left, right, preferred_element_type=jnp.float32)]
    unnamed x363 -> x345, local copies, waits for them, and re-layouts: 20.8 us -> 22.1 us
  transfers between devices with their start and end apart: 75 -> 74, of which waited for: 27 -> 27; matrix products, arithmetic and copies ran while one was open for 27% -> 27% of each run, Pallas kernels for 9% -> 10%
where the time goes in v2:
time: 605 us; the launch traced here: 595 us
  starting transfers between devices  124 us (20%)
  waiting for transfers between devices  93.9 us (16%)
  blocking collectives  88.2 us (15%)
  matrix products  82.5 us (14%)
  local copies, waits for them, and re-layouts  70.1 us (12%)
  Pallas kernels  59.7 us (10%)
  other arithmetic  58.9 us (10%)
  between operations  17 us (3%)
    all_gather x3, blocking collectives, spread(): return lax.all_gather(value, 'tp', axis=0, tiled=True)  58.9 us
    ppermute x30, starting transfers between devices, partner(): got = lax.ppermute(value, axis, [(s, s ^ 1 << bit) for s in range(count)])  54.4 us
    dot_general x17, matrix products, matmul(): return jnp.dot(left, right, preferred_element_type=jnp.float32)  38 us
    pallas_call x4, Pallas kernels, kernel_call(): pl.pallas_call(body, out_shape=outs, in_specs=[pl.BlockSpec(memory_space=...  35.2 us
    ppermute x30, waiting for transfers between devices, partner(): got = lax.ppermute(value, axis, [(s, s ^ 1 << bit) for s in range(count)])  33.9 us
    dot_general x11, matrix products, matmul_nt(): lax.dot_general(left, right, (((1,), (1,)), ((), ())), preferred_element_...  27.7 us
    unnamed x345, local copies, waits for them, and re-layouts  22.1 us
    ppermute x15, waiting for transfers between devices, received(): lax.ppermute(sent, axis, [(s, (s + shift) % count) for s in range(count)])  20.8 us
  transfers between devices with their start and end apart: 74, of which 27 were waited for; matrix products, arithmetic and copies ran while one was open for 27% of the time, Pallas kernels for 10%

profile of v2, /device:TPU:0, one launch (start us, length us, event | category | flops | bytes accessed | tf_op | source)
XLA Modules:
  0.0 594.7 jit_solution(12416133550259578610)
XLA Ops:
  10.2 22.2 %all_gather.30 = bf16[256,1600]{1,0:T(8,128)(2,1)S(1)} all-gather(bf16[64,1600]{1,0:T(8,128)(2,1)S(1)} %copy-done.51), channel_id=1, replica_groups=mesh['seq'=8,'tp'=4] {'tp'}, dimensions={0}, use_global_device_ids=true | all-gather | bytes 1024000 | tf_op jit(solution)/shard_map/all_gather | solution.py:716
  37.2 6.7 %all-gather.6.cloned.1.call-done = bf16[1600,800]{1,0:T(8,128)(2,1)} async-done(((bf16[200,800]{1,0:T(8,128)(2,1)}), bf16[1600,800]{1,0:T(8,128)(2,1)}) %all-gather.6.cloned.1.call-update) | async-done | bytes 2560016 | tf_op jit(solution)/shard_map/all_gather | solution.py:739
  59.2 7.0 %collective-permute-done.2 = bf16[256,160]{1,0:T(8,128)(2,1)S(1)} collective-permute-done((bf16[256,160]{1,0:T(8,128)(2,1)S(1)}, bf16[256,160]{1,0:T(8,128)(2,1)S(1)}, u32[]{:S(2)}, u32[]{:S(2)}) %collective-permute-start.2) | collective-permute-done | bytes 81952 | tf_op jit(solution)/shard_map/ppermute | solution.py:637
  76.2 4.5 collective-permute-start.5
  80.9 7.0 %collective-permute-done.5 = bf16[256,132]{1,0:T(8,128)(2,1)S(1)} collective-permute-done((bf16[256,132]{1,0:T(8,128)(2,1)S(1)}, bf16[256,132]{1,0:T(8,128)(2,1)S(1)}, u32[]{:S(2)}, u32[]{:S(2)}) %collective-permute-start.5) | collective-permute-done | bytes 67616 | tf_op jit(solution)/shard_map/ppermute | solution.py:497
  100.1 16.9 %all-gather = f32[192,800]{1,0:T(8,128)} all-gather(f32[24,800]{1,0:T(8,128)S(1)} %shard_map.407), channel_id=2, replica_groups=mesh['seq'=8,'tp'=4] {'seq'}, dimensions={0}, use_global_device_ids=true | all-gather | bytes 691200 | tf_op jit(solution)/shard_map/all_gather | solution.py:824
  119.2 4.2 collective-permute-start.12
  139.2 9.7 %shard_map.408 = (f32[256,800]{1,0:T(8,128)S(1)}, bf16[4112,800]{1,0:T(8,128)(2,1)}) custom-call(s32[1]{0:T(128)} %bitcast.6.place_ref, f32[8,24,800]{2,1,0:T(8,128)S(1)} %bitcast.219, f32[256,800]{1,0:T(8,128)S(1)} %copy-done.14, f32[256,800]{1,0:T(8,128)S(1)} %get-tuple-element.131.drive_in.drive_ref, f32[256,16,128]{2,1,0:T(8,128)S(1)} %copy-done.6, ...), custom_call_target="tpu_custom_call" | custom-call | flops 19660800 | bytes 9011200 | tf_op jit(solution)/shard_map/pallas_call | solution.py:251
  152.3 4.1 multiply_convert_fusion.1
  164.8 5.1 collective-permute-start.23
  169.9 11.1 %shard_map.409 = (bf16[5,320,1280]{2,1,0:T(8,128)(2,1)}, bf16[5,320,64]{2,1,0:T(8,128)(2,1)S(1)}) custom-call(bf16[4,256,160]{2,1,0:T(8,128)(2,1)} %collective-permute-done.7.refs_0_, bf16[4,256,160]{2,1,0:T(8,128)(2,1)} %collective-permute-done.11.refs_1_, bf16[4,256,160]{2,1,0:T(8,128)(2,1)} %collective-permute-done.12.refs_2_, ...), custom_call_target="tpu_custom_call" | custom-call | flops 524288000 | bytes 4505600 | tf_op jit(solution)/shard_map/pallas_call | solution.py:436
  197.6 4.3 collective-permute-done.22
  202.0 6.2 %collective-permute-done.21 = bf16[64,1600]{1,0:T(8,128)(2,1)S(1)} collective-permute-done((bf16[64,1600]{1,0:T(8,128)(2,1)S(1)}, bf16[64,1600]{1,0:T(8,128)(2,1)S(1)}, u32[]{:S(2)}, u32[]{:S(2)}) %collective-permute-start.21) | collective-permute-done | bytes 204832 | tf_op jit(solution)/shard_map/ppermute | solution.py:868
  211.0 18.5 %all_gather.36 = bf16[256,1664]{1,0:T(8,128)(2,1)S(1)} all-gather(bf16[64,1664]{1,0:T(8,128)(2,1)S(1)} %pad.102), channel_id=1, replica_groups=mesh['seq'=8,'tp'=4] {'tp'}, dimensions={0}, use_global_device_ids=true | all-gather | bytes 1064960 | tf_op jit(solution)/shard_map/all_gather | solution.py:716
  229.5 12.3 %collective-permute-start.24 = (bf16[256,1664]{1,0:T(8,128)(2,1)S(1)}, bf16[256,1664]{1,0:T(8,128)(2,1)S(1)}, u32[]{:S(2)}, u32[]{:S(2)}) collective-permute-start(bf16[256,1664]{1,0:T(8,128)(2,1)S(1)} %all_gather.36), channel_id=1, source_target_pairs={{0,4},{4,0},{8,12},{12,8},{16,20},{20,16},{24,28},{28,24},{1,5},{5... | collective-permute-start | bytes 2555912 | tf_op jit(solution)/shard_map/ppermute | solution.py:497
  243.8 5.2 fusion.4
  260.7 4.9 fusion.10
  265.6 4.5 convolution_convert_fusion
  295.9 5.8 collective-permute-done.28
  310.3 18.2 %all_gather.37 = bf16[256,1600]{1,0:T(8,128)(2,1)S(1)} all-gather(bf16[64,1600]{1,0:T(8,128)(2,1)S(1)} %get-tuple-element.296), channel_id=1, replica_groups=mesh['seq'=8,'tp'=4] {'tp'}, dimensions={0}, use_global_device_ids=true | all-gather | bytes 1024000 | tf_op jit(solution)/shard_map/all_gather | solution.py:716
  339.0 4.5 all-to-all-start.1
  349.2 12.4 %all-gather.1 = f32[192,800]{1,0:T(8,128)} all-gather(f32[24,800]{1,0:T(8,128)S(1)} %shard_map.410), channel_id=3, replica_groups=mesh['seq'=8,'tp'=4] {'seq'}, dimensions={0}, use_global_device_ids=true | all-gather | bytes 691200 | tf_op jit(solution)/shard_map/all_gather | solution.py:931
  361.6 4.1 fusion.19
  375.2 4.4 all-to-all-start.2
  391.0 13.3 %shard_map.412 = (bf16[5,320,64]{2,1,0:T(8,128)(2,1)S(1)}, bf16[4,160,1280]{2,1,0:T(8,128)(2,1)}) custom-call(bf16[4,256,160]{2,1,0:T(8,128)(2,1)} %collective-permute-done.7.refs_0_, bf16[4,256,160]{2,1,0:T(8,128)(2,1)} %collective-permute-done.11.refs_1_, bf16[4,256,160]{2,1,0:T(8,128)(2,1)} %collective-permute-done.12.refs_2_, ...), custom_call_target="tpu_custom_call" | custom-call | flops 1048576000 | bytes 8192000 | tf_op jit(solution)/shard_map/pallas_call | solution.py:464
  409.6 19.1 %shard_map.411 = (f32[256,800]{1,0:T(8,128)S(1)}, f32[256,800]{1,0:T(8,128)S(1)}, f32[16,256]{1,0:T(8,128)S(1)}, f32[16,256]{1,0:T(8,128)S(1)}, f32[16,800]{1,0:T(8,128)S(1)}) custom-call(s32[1]{0:T(128)} %bitcast.6.place_ref, f32[8,24,800]{2,1,0:T(8,128)S(1)} %bitcast.215, f32[256,800]{1,0:T(8,128)S(1)} %copy-done.16, f32[256,800]{1,0:T(8,128)S(1)} %copy-done.12, ...), custom_call_target="tpu_custom_call" | custom-call | flops 39321600 | bytes 9011200 | tf_op jit(solution)/shard_map/pallas_call | solution.py:251
  485.5 5.3 collective-permute-done.42
  520.8 13.0 %collective-permute-done.47 = bf16[64,1600]{1,0:T(8,128)(2,1)S(1)} collective-permute-done((bf16[64,1600]{1,0:T(8,128)(2,1)S(1)}, bf16[64,1600]{1,0:T(8,128)(2,1)S(1)}, u32[]{:S(2)}, u32[]{:S(2)}) %collective-permute-start.47) | collective-permute-done | bytes 204832 | tf_op jit(solution)/shard_map/ppermute | solution.py:609
  551.5 4.6 collective-permute-done.57
  560.7 5.7 collective-permute-done.52
  567.9 4.7 collective-permute-done.55
  573.5 4.4 convert_bitcast_fusion
  (687 shorter events, 303.8 us)
Async XLA Ops:
  7.2 36.6 %all-gather.6.cloned.1.call-start = ((), (), s32[]{:S(2)}) async-start(), calls=%async_computation.6 | async-start | bytes 3225600 | tf_op jit(solution)/shard_map/all_gather | solution.py:739
  8.0 87.6 %all-gather.8.cloned.1.call-start = ((), (), s32[]{:S(2)}) async-start(), calls=%async_computation.7 | async-start | bytes 6451200 | tf_op jit(solution)/shard_map/all_gather | solution.py:739
  10.1 198.3 %all-gather.10.cloned.1.call-start = ((), (), s32[]{:S(2)}) async-start(), calls=%async_computation.8 | async-start | bytes 9216000 | tf_op jit(solution)/shard_map/all_gather | solution.py:742
  88.7 45.7 %collective-permute-start.8 = (bf16[64,1664]{1,0:T(8,128)(2,1)}, bf16[64,1664]{1,0:T(8,128)(2,1)}, u32[]{:S(2)}, u32[]{:S(2)}) collective-permute-start(bf16[64,1664]{1,0:T(8,128)(2,1)} %get-tuple-element.313), channel_id=1, source_target_pairs={{0,1},{1,2},{2,3},{3,0},{4,5},{5,6},{6,7},{7,4},{8,9},{9,10},{10,1... | collective-permute-start | bytes 638984 | tf_op jit(solution)/shard_map/ppermute | solution.py:637
  88.7 43.6 %collective-permute-start.9 = (bf16[64,1664]{1,0:T(8,128)(2,1)}, bf16[64,1664]{1,0:T(8,128)(2,1)}, u32[]{:S(2)}, u32[]{:S(2)}) collective-permute-start(bf16[64,1664]{1,0:T(8,128)(2,1)} %get-tuple-element.313), channel_id=1, source_target_pairs={{0,2},{1,3},{2,0},{3,1},{4,6},{5,7},{6,4},{7,5},{8,10},{9,11},{10,... | collective-permute-start | bytes 638984 | tf_op jit(solution)/shard_map/ppermute | solution.py:637
  91.4 37.9 %collective-permute-start.10 = (bf16[64,1664]{1,0:T(8,128)(2,1)}, bf16[64,1664]{1,0:T(8,128)(2,1)}, u32[]{:S(2)}, u32[]{:S(2)}) collective-permute-start(bf16[64,1664]{1,0:T(8,128)(2,1)} %get-tuple-element.313), channel_id=1, source_target_pairs={{0,3},{1,0},{2,1},{3,2},{4,7},{5,4},{6,5},{7,6},{8,11},{9,8},{10,9... | collective-permute-start | bytes 638984 | tf_op jit(solution)/shard_map/ppermute | solution.py:637
  116.9 43.2 %collective-permute-start.13 = (bf16[4,256,160]{2,1,0:T(8,128)(2,1)S(1)}, bf16[4,256,160]{2,1,0:T(8,128)(2,1)S(1)}, u32[]{:S(2)}, u32[]{:S(2)}) collective-permute-start(bf16[4,256,160]{2,1,0:T(8,128)(2,1)S(1)} %pad_maximum_fusion.14.refs_4_), channel_id=1, source_target_pairs={{0,4},{4,8},{8,12},{12,16},{16,20},{20,24},{24,28},{1,5},{5,9},{9,... | collective-permute-start | bytes 983048 | tf_op jit(solution)/shard_map/ppermute | solution.py:488
  119.2 43.2 %collective-permute-start.12 = (bf16[4,256,160]{2,1,0:T(8,128)(2,1)S(1)}, bf16[4,256,160]{2,1,0:T(8,128)(2,1)}, u32[]{:S(2)}, u32[]{:S(2)}) collective-permute-start(bf16[4,256,160]{2,1,0:T(8,128)(2,1)S(1)} %pad_maximum_fusion.14.refs_4_), channel_id=1, source_target_pairs={{0,8},{4,12},{8,16},{12,20},{16,24},{20,28},{1,9},{5,13},{9,17},{1... | collective-permute-start | bytes 983048 | tf_op jit(solution)/shard_map/ppermute | solution.py:488
  125.2 38.1 %all-to-all-start = ((bf16[4,64,400]{2,1,0:T(8,128)(2,1)}), bf16[4,64,400]{2,1,0:T(8,128)(2,1)}, u32[]{:S(2)}, u32[]{:S(2)}) async-start(bf16[4,64,400]{2,1,0:T(8,128)(2,1)} %bitcast.250), calls=%async_computation | async-start | bytes 524288 | tf_op jit(solution)/shard_map/all_to_all | solution.py:629
  129.2 275.8 %reduce-scatter.3.cloned.1.call-start = ((), (), s32[]{:S(2)}) async-start(), calls=%async_computation.9 | async-start | bytes 6144000 | tf_op jit(solution)/shard_map/reduce_scatter | solution.py:747
  129.3 35.5 %collective-permute-start.11 = (bf16[4,256,160]{2,1,0:T(8,128)(2,1)S(1)}, bf16[4,256,160]{2,1,0:T(8,128)(2,1)}, u32[]{:S(2)}, u32[]{:S(2)}) collective-permute-start(bf16[4,256,160]{2,1,0:T(8,128)(2,1)S(1)} %pad_maximum_fusion.14.refs_4_), channel_id=1, source_target_pairs={{0,12},{4,16},{8,20},{12,24},{16,28},{1,13},{5,17},{9,21},{13,25},... | collective-permute-start | bytes 983048 | tf_op jit(solution)/shard_map/ppermute | solution.py:488
  132.3 37.6 %collective-permute-start.7 = (bf16[4,256,160]{2,1,0:T(8,128)(2,1)S(1)}, bf16[4,256,160]{2,1,0:T(8,128)(2,1)}, u32[]{:S(2)}, u32[]{:S(2)}) collective-permute-start(bf16[4,256,160]{2,1,0:T(8,128)(2,1)S(1)} %pad_maximum_fusion.14.refs_4_), channel_id=1, source_target_pairs={{0,16},{4,20},{8,24},{12,28},{1,17},{5,21},{9,25},{13,29},{2,18},{... | collective-permute-start | bytes 983048 | tf_op jit(solution)/shard_map/ppermute | solution.py:488
  158.6 24.2 %collective-permute-start.17 = (bf16[64,1600]{1,0:T(8,128)(2,1)}, bf16[64,1600]{1,0:T(8,128)(2,1)S(1)}, u32[]{:S(2)}, u32[]{:S(2)}) collective-permute-start(bf16[64,1600]{1,0:T(8,128)(2,1)} %get-tuple-element.276), channel_id=1, source_target_pairs={{0,1},{1,2},{2,3},{3,0},{4,5},{5,6},{6,7},{7,4},{8,9},{9,10},{10,1... | collective-permute-start | bytes 614408 | tf_op jit(solution)/shard_map/ppermute | solution.py:609
  160.2 24.6 %collective-permute-start.19 = (bf16[64,1600]{1,0:T(8,128)(2,1)}, bf16[64,1600]{1,0:T(8,128)(2,1)}, u32[]{:S(2)}, u32[]{:S(2)}) collective-permute-start(bf16[64,1600]{1,0:T(8,128)(2,1)} %get-tuple-element.277), channel_id=1, source_target_pairs={{0,3},{1,0},{2,1},{3,2},{4,7},{5,4},{6,5},{7,6},{8,11},{9,8},{10,9... | collective-permute-start | bytes 614408 | tf_op jit(solution)/shard_map/ppermute | solution.py:609
  162.4 24.3 %collective-permute-start.18 = (bf16[64,1600]{1,0:T(8,128)(2,1)}, bf16[64,1600]{1,0:T(8,128)(2,1)}, u32[]{:S(2)}, u32[]{:S(2)}) collective-permute-start(bf16[64,1600]{1,0:T(8,128)(2,1)} %get-tuple-element.278), channel_id=1, source_target_pairs={{0,2},{1,3},{2,0},{3,1},{4,6},{5,7},{6,4},{7,5},{8,10},{9,11},{10,... | collective-permute-start | bytes 614408 | tf_op jit(solution)/shard_map/ppermute | solution.py:609
  164.8 43.8 %collective-permute-start.23 = (bf16[256,1664]{1,0:T(8,128)(2,1)}, bf16[256,1664]{1,0:T(8,128)(2,1)}, u32[]{:S(2)}, u32[]{:S(2)}) collective-permute-start(bf16[256,1664]{1,0:T(8,128)(2,1)} %bitcast.256), channel_id=1, source_target_pairs={{0,4},{4,0},{8,12},{12,8},{16,20},{20,16},{24,28},{28,24},{1,5},{5... | collective-permute-start | bytes 2555912 | tf_op jit(solution)/shard_map/ppermute | solution.py:497
  292.9 74.9 %collective-permute-start.37 = (bf16[2,400,768]{2,1,0:T(8,128)(2,1)}, bf16[2,400,768]{2,1,0:T(8,128)(2,1)}, u32[]{:S(2)}, u32[]{:S(2)}) collective-permute-start(bf16[2,400,768]{2,1,0:T(8,128)(2,1)} %dynamic-slice_bitcast_fusion), channel_id=1, source_target_pairs={{0,16},{4,20},{8,24},{12,28},{16,0},{20,4},{24,8},{28,12},{1,17},{... | collective-permute-start | bytes 3686408 | tf_op jit(solution)/shard_map/ppermute | solution.py:497
  335.1 103.1 %collective-permute-start.34 = (bf16[64,1600]{1,0:T(8,128)(2,1)}, bf16[64,1600]{1,0:T(8,128)(2,1)}, u32[]{:S(2)}, u32[]{:S(2)}) collective-permute-start(bf16[64,1600]{1,0:T(8,128)(2,1)} %get-tuple-element.267), channel_id=1, source_target_pairs={{0,3},{1,0},{2,1},{3,2},{4,7},{5,4},{6,5},{7,6},{8,11},{9,8},{10,9... | collective-permute-start | bytes 614408 | tf_op jit(solution)/shard_map/ppermute | solution.py:609
  337.4 96.7 %collective-permute-start.33 = (bf16[64,1600]{1,0:T(8,128)(2,1)}, bf16[64,1600]{1,0:T(8,128)(2,1)}, u32[]{:S(2)}, u32[]{:S(2)}) collective-permute-start(bf16[64,1600]{1,0:T(8,128)(2,1)} %get-tuple-element.268), channel_id=1, source_target_pairs={{0,2},{1,3},{2,0},{3,1},{4,6},{5,7},{6,4},{7,5},{8,10},{9,11},{10,... | collective-permute-start | bytes 614408 | tf_op jit(solution)/shard_map/ppermute | solution.py:609
  337.4 98.7 %collective-permute-start.32 = (bf16[64,1600]{1,0:T(8,128)(2,1)}, bf16[64,1600]{1,0:T(8,128)(2,1)}, u32[]{:S(2)}, u32[]{:S(2)}) collective-permute-start(bf16[64,1600]{1,0:T(8,128)(2,1)} %get-tuple-element.269), channel_id=1, source_target_pairs={{0,1},{1,2},{2,3},{3,0},{4,5},{5,6},{6,7},{7,4},{8,9},{9,10},{10,1... | collective-permute-start | bytes 614408 | tf_op jit(solution)/shard_map/ppermute | solution.py:609
  339.0 33.5 %all-to-all-start.1 = ((bf16[4,64,1600]{2,1,0:T(8,128)(2,1)}), bf16[4,64,1600]{2,1,0:T(8,128)(2,1)}, u32[]{:S(2)}, u32[]{:S(2)}) async-start(bf16[4,64,1600]{2,1,0:T(8,128)(2,1)} %broadcast_in_dim.28), calls=%async_computation.1 | async-start | bytes 1703936 | tf_op jit(solution)/shard_map/all_to_all | solution.py:629
  345.3 37.3 %collective-permute-start.31 = (bf16[800,800]{1,0:T(8,128)(2,1)}, bf16[800,800]{1,0:T(8,128)(2,1)}, u32[]{:S(2)}, u32[]{:S(2)}) collective-permute-start(bf16[800,800]{1,0:T(8,128)(2,1)} %convolution_convert_fusion.7), channel_id=1, source_target_pairs={{0,4},{4,0},{8,12},{12,8},{16,20},{20,16},{24,28},{28,24},{1,5},{5... | collective-permute-start | bytes 3840008 | tf_op jit(solution)/shard_map/ppermute | solution.py:497
  379.6 87.9 %reduce-scatter.5.cloned.1.call-start = ((), (), s32[]{:S(2)}) async-start(), calls=%async_computation.10 | async-start | bytes 2048000 | tf_op jit(solution)/shard_map/reduce_scatter | solution.py:945
  382.5 85.0 %collective-permute-start.62 = (bf16[400,768]{1,0:T(8,128)(2,1)}, bf16[400,768]{1,0:T(8,128)(2,1)}, u32[]{:S(2)}, u32[]{:S(2)}) collective-permute-start(bf16[400,768]{1,0:T(8,128)(2,1)} %dynamic-slice_bitcast_fusion.6), channel_id=1, source_target_pairs={{0,8},{4,12},{8,0},{12,4},{16,24},{20,28},{24,16},{28,20},{1,9},{5... | collective-permute-start | bytes 1843208 | tf_op jit(solution)/shard_map/ppermute | solution.py:497
  387.6 79.9 %collective-permute-start.40 = (bf16[2,200,800]{2,1,0:T(8,128)(2,1)}, bf16[2,200,800]{2,1,0:T(8,128)(2,1)}, u32[]{:S(2)}, u32[]{:S(2)}) collective-permute-start(bf16[2,200,800]{2,1,0:T(8,128)(2,1)} %dynamic-slice_bitcast_fusion.2), channel_id=1, source_target_pairs={{0,8},{4,12},{8,0},{12,4},{16,24},{20,28},{24,16},{28,20},{1,9},{5... | collective-permute-start | bytes 1920008 | tf_op jit(solution)/shard_map/ppermute | solution.py:497
  436.1 42.5 %collective-permute-start.39 = (bf16[2,200,800]{2,1,0:T(8,128)(2,1)}, bf16[2,200,800]{2,1,0:T(8,128)(2,1)}, u32[]{:S(2)}, u32[]{:S(2)}) collective-permute-start(bf16[2,200,800]{2,1,0:T(8,128)(2,1)} %dynamic-slice_bitcast_fusion.3), channel_id=1, source_target_pairs={{0,16},{4,20},{8,24},{12,28},{16,0},{20,4},{24,8},{28,12},{1,17},{... | collective-permute-start | bytes 1920008 | tf_op jit(solution)/shard_map/ppermute | solution.py:497
  452.5 121.0 %all-reduce.25.cloned.1.call-start = ((), (), s32[]{:S(2)}) async-start(), calls=%async_computation.11 | async-start | bytes 5324800 | tf_op jit(solution)/shard_map/psum | solution.py:951
  467.6 46.1 %collective-permute-start.61 = (bf16[200,1536]{1,0:T(8,128)(2,1)}, bf16[200,1536]{1,0:T(8,128)(2,1)}, u32[]{:S(2)}, u32[]{:S(2)}) collective-permute-start(bf16[200,1536]{1,0:T(8,128)(2,1)} %dynamic-slice_bitcast_fusion.5), channel_id=1, source_target_pairs={{0,4},{4,0},{8,12},{12,8},{16,20},{20,16},{24,28},{28,24},{1,5},{5... | collective-permute-start | bytes 1843208 | tf_op jit(solution)/shard_map/ppermute | solution.py:497
  498.1 43.0 %collective-permute-start.59 = (bf16[200,800]{1,0:T(8,128)(2,1)}, bf16[200,800]{1,0:T(8,128)(2,1)}, u32[]{:S(2)}, u32[]{:S(2)}) collective-permute-start(bf16[200,800]{1,0:T(8,128)(2,1)} %dynamic-slice_bitcast_fusion.8), channel_id=1, source_target_pairs={{0,16},{4,20},{8,24},{12,28},{16,0},{20,4},{24,8},{28,12},{1,17},{... | collective-permute-start | bytes 960008 | tf_op jit(solution)/shard_map/ppermute | solution.py:497
  501.6 39.5 %collective-permute-start.60 = (bf16[200,800]{1,0:T(8,128)(2,1)}, bf16[200,800]{1,0:T(8,128)(2,1)}, u32[]{:S(2)}, u32[]{:S(2)}) collective-permute-start(bf16[200,800]{1,0:T(8,128)(2,1)} %dynamic-slice_bitcast_fusion.9), channel_id=1, source_target_pairs={{0,8},{4,12},{8,0},{12,4},{16,24},{20,28},{24,16},{28,20},{1,9},{5... | collective-permute-start | bytes 960008 | tf_op jit(solution)/shard_map/ppermute | solution.py:497
  513.6 20.2 %collective-permute-start.47 = (bf16[64,1600]{1,0:T(8,128)(2,1)S(1)}, bf16[64,1600]{1,0:T(8,128)(2,1)S(1)}, u32[]{:S(2)}, u32[]{:S(2)}) collective-permute-start(bf16[64,1600]{1,0:T(8,128)(2,1)S(1)} %get-tuple-element.264), channel_id=1, source_target_pairs={{0,2},{1,3},{2,0},{3,1},{4,6},{5,7},{6,4},{7,5},{8,10},{9,11},{10,... | collective-permute-start | bytes 614408 | tf_op jit(solution)/shard_map/ppermute | solution.py:609
  519.3 36.8 %collective-permute-start.54 = (bf16[2,200,800]{2,1,0:T(8,128)(2,1)}, bf16[2,200,800]{2,1,0:T(8,128)(2,1)}, u32[]{:S(2)}, u32[]{:S(2)}) collective-permute-start(bf16[2,200,800]{2,1,0:T(8,128)(2,1)} %dynamic-slice_bitcast_fusion.1), channel_id=1, source_target_pairs={{0,16},{4,20},{8,24},{12,28},{16,0},{20,4},{24,8},{28,12},{1,17},{... | collective-permute-start | bytes 1920008 | tf_op jit(solution)/shard_map/ppermute | solution.py:497
  (214 other events, 2199.1 us)
Sparse Core Ops, SparseCore 0:
  9.9 33.8 all-gather.5
  46.3 43.2 all-gather.7
  92.0 111.8 all-gather.9
  270.3 82.3 reduce-scatter.2
  405.2 38.8 reduce-scatter.4
  463.0 80.5 all-reduce.24

commit v3 on v2

--- a/solution.py
+++ b/solution.py
@@ -1016,16 +1016,10 @@
     block_in_low = row_major(grad_block_in.astype(jnp.bfloat16))
     block_in_pieces = received(block_in_low.reshape(tp_count, quarter, -1), "tp")
     proj_sum = proj_x.finish()
-    grad_mixer_in = sum(
-        after(piece, tail).astype(jnp.float32) for piece in block_in_pieces
-    )
-    stream_grad = (grad_resid + rms_back(grad_mixer_in * mixer_gain, normed_one, scale_one)).astype(
-        jnp.bfloat16
-    )
     grad_mixer_gain = jnp.sum(after(grad_block_in, tail) * block_normed, 0)
     gain_parts = jnp.stack([grad_mixer_gain, grad_attn_gain, grad_mamba_gain, grad_ffn_gain])
     gain_parts = all_sum(gain_parts, ("tp",), jnp.float32)
-    grad_select = matmul_tn(grad_selected, mixed_low)
+    grad_select = matmul_tn(after(grad_selected, tail), mixed_low)
     grad_conv_bias = jnp.sum(grad_conv, 0)
     lone_rows = [
         jnp.sum(grad_conv * padded[tap : tap + rows] * taps[tap], 0) for tap in range(CONV)
@@ -1052,6 +1046,12 @@
     zgate_sum = zgate_x.finish(tail)
     gate_grad, up_grad = core_rows_back(gate_up_sum, 2, half, tail)
     (down_grad,) = core_rows_back(down_sum, 1, half, tail)
+    grad_mixer_in = sum(
+        after(piece, gate_grad, up_grad, down_grad, mout_sum, zgate_sum).astype(jnp.float32) for piece in block_in_pieces
+    )
+    stream_grad = (grad_resid + rms_back(grad_mixer_in * mixer_gain, normed_one, scale_one)).astype(
+        jnp.bfloat16
+    )
     head_sums = after(head_sums, proj_sum)
     ranks = STEP_RANK + 2 * STATE
     starts = [0]

time: 605 us -> 600 us (level)
  waiting for transfers between devices: 93.9 us -> 84.9 us
    ppermute x15, waiting for transfers between devices: 20.8 us -> 9.79 us  [received(): lax.ppermute(sent, axis, [(s, (s + shift) % count) for s in range(count)])]
    unnamed x345 -> x355, local copies, waits for them, and re-layouts: 22.1 us -> 23.5 us
  transfers between devices with their start and end apart: 74 -> 74, of which waited for: 27 -> 22; matrix products, arithmetic and copies ran while one was open for 27% -> 28% of each run, Pallas kernels for 10% -> 10%
where the time goes in v3:
time: 600 us; the launch traced here: 590 us
  starting transfers between devices  121 us (20%)
  blocking collectives  88.2 us (15%)
  waiting for transfers between devices  84.9 us (14%)
  matrix products  83.2 us (14%)
  local copies, waits for them, and re-layouts  74.7 us (12%)
  other arithmetic  60.9 us (10%)
  Pallas kernels  59.7 us (10%)
  between operations  17 us (3%)
    all_gather x3, blocking collectives, spread(): return lax.all_gather(value, 'tp', axis=0, tiled=True)  58.9 us
    ppermute x30, starting transfers between devices, partner(): got = lax.ppermute(value, axis, [(s, s ^ 1 << bit) for s in range(count)])  51.2 us
    dot_general x17, matrix products, matmul(): return jnp.dot(left, right, preferred_element_type=jnp.float32)  38 us
    pallas_call x4, Pallas kernels, kernel_call(): pl.pallas_call(body, out_shape=outs, in_specs=[pl.BlockSpec(memory_space=...  35.2 us
    ppermute x30, waiting for transfers between devices, partner(): got = lax.ppermute(value, axis, [(s, s ^ 1 << bit) for s in range(count)])  33.5 us
    dot_general x11, matrix products, matmul_nt(): lax.dot_general(left, right, (((1,), (1,)), ((), ())), preferred_element_...  28.7 us
    unnamed x355, local copies, waits for them, and re-layouts  23.5 us
    ppermute x15, starting transfers between devices, received(): lax.ppermute(sent, axis, [(s, (s + shift) % count) for s in range(count)])  19.9 us
  transfers between devices with their start and end apart: 74, of which 22 were waited for; matrix products, arithmetic and copies ran while one was open for 28% of the time, Pallas kernels for 10%

profile of v3, /device:TPU:0, one launch (start us, length us, event | category | flops | bytes accessed | tf_op | source)
XLA Modules:
  0.0 590.0 jit_solution(16802995665017810110)
XLA Ops:
  10.2 22.2 %all_gather.30 = bf16[256,1600]{1,0:T(8,128)(2,1)S(1)} all-gather(bf16[64,1600]{1,0:T(8,128)(2,1)S(1)} %copy-done.52), channel_id=1, replica_groups=mesh['seq'=8,'tp'=4] {'tp'}, dimensions={0}, use_global_device_ids=true | all-gather | bytes 1024000 | tf_op jit(solution)/shard_map/all_gather | solution.py:716
  37.2 6.7 %all-gather.6.cloned.1.call-done = bf16[1600,800]{1,0:T(8,128)(2,1)} async-done(((bf16[200,800]{1,0:T(8,128)(2,1)}), bf16[1600,800]{1,0:T(8,128)(2,1)}) %all-gather.6.cloned.1.call-update) | async-done | bytes 2560016 | tf_op jit(solution)/shard_map/all_gather | solution.py:739
  59.2 7.0 %collective-permute-done.2 = bf16[256,160]{1,0:T(8,128)(2,1)S(1)} collective-permute-done((bf16[256,160]{1,0:T(8,128)(2,1)S(1)}, bf16[256,160]{1,0:T(8,128)(2,1)S(1)}, u32[]{:S(2)}, u32[]{:S(2)}) %collective-permute-start.2) | collective-permute-done | bytes 81952 | tf_op jit(solution)/shard_map/ppermute | solution.py:637
  76.2 4.5 collective-permute-start.5
  80.9 7.0 %collective-permute-done.5 = bf16[256,132]{1,0:T(8,128)(2,1)S(1)} collective-permute-done((bf16[256,132]{1,0:T(8,128)(2,1)S(1)}, bf16[256,132]{1,0:T(8,128)(2,1)S(1)}, u32[]{:S(2)}, u32[]{:S(2)}) %collective-permute-start.5) | collective-permute-done | bytes 67616 | tf_op jit(solution)/shard_map/ppermute | solution.py:497
  100.0 16.9 %all-gather = f32[192,800]{1,0:T(8,128)} all-gather(f32[24,800]{1,0:T(8,128)S(1)} %shard_map.407), channel_id=2, replica_groups=mesh['seq'=8,'tp'=4] {'seq'}, dimensions={0}, use_global_device_ids=true | all-gather | bytes 691200 | tf_op jit(solution)/shard_map/all_gather | solution.py:824
  119.2 4.2 collective-permute-start.12
  125.2 4.0 all-to-all-start
  139.2 9.7 %shard_map.408 = (f32[256,800]{1,0:T(8,128)S(1)}, bf16[4112,800]{1,0:T(8,128)(2,1)}) custom-call(s32[1]{0:T(128)} %bitcast.6.place_ref, f32[8,24,800]{2,1,0:T(8,128)S(1)} %bitcast.219, f32[256,800]{1,0:T(8,128)S(1)} %copy-done.14, f32[256,800]{1,0:T(8,128)S(1)} %get-tuple-element.132.drive_in.drive_ref, f32[256,16,128]{2,1,0:T(8,128)S(1)} %copy-done.6, ...), custom_call_target="tpu_custom_call" | custom-call | flops 19660800 | bytes 9011200 | tf_op jit(solution)/shard_map/pallas_call | solution.py:251
  152.2 4.2 multiply_convert_fusion.1
  164.7 5.1 collective-permute-start.23
  169.9 11.2 %shard_map.409 = (bf16[5,320,1280]{2,1,0:T(8,128)(2,1)}, bf16[5,320,64]{2,1,0:T(8,128)(2,1)S(1)}) custom-call(bf16[4,256,160]{2,1,0:T(8,128)(2,1)} %collective-permute-done.7.refs_0_, bf16[4,256,160]{2,1,0:T(8,128)(2,1)} %collective-permute-done.11.refs_1_, bf16[4,256,160]{2,1,0:T(8,128)(2,1)} %collective-permute-done.12.refs_2_, ...), custom_call_target="tpu_custom_call" | custom-call | flops 524288000 | bytes 4505600 | tf_op jit(solution)/shard_map/pallas_call | solution.py:436
  197.6 4.3 collective-permute-done.22
  202.0 6.2 %collective-permute-done.21 = bf16[64,1600]{1,0:T(8,128)(2,1)S(1)} collective-permute-done((bf16[64,1600]{1,0:T(8,128)(2,1)S(1)}, bf16[64,1600]{1,0:T(8,128)(2,1)S(1)}, u32[]{:S(2)}, u32[]{:S(2)}) %collective-permute-start.21) | collective-permute-done | bytes 204832 | tf_op jit(solution)/shard_map/ppermute | solution.py:868
  211.0 18.5 %all_gather.36 = bf16[256,1664]{1,0:T(8,128)(2,1)S(1)} all-gather(bf16[64,1664]{1,0:T(8,128)(2,1)S(1)} %pad.102), channel_id=1, replica_groups=mesh['seq'=8,'tp'=4] {'tp'}, dimensions={0}, use_global_device_ids=true | all-gather | bytes 1064960 | tf_op jit(solution)/shard_map/all_gather | solution.py:716
  229.5 12.3 %collective-permute-start.24 = (bf16[256,1664]{1,0:T(8,128)(2,1)S(1)}, bf16[256,1664]{1,0:T(8,128)(2,1)S(1)}, u32[]{:S(2)}, u32[]{:S(2)}) collective-permute-start(bf16[256,1664]{1,0:T(8,128)(2,1)S(1)} %all_gather.36), channel_id=1, source_target_pairs={{0,4},{4,0},{8,12},{12,8},{16,20},{20,16},{24,28},{28,24},{1,5},{5... | collective-permute-start | bytes 2555912 | tf_op jit(solution)/shard_map/ppermute | solution.py:497
  243.8 5.2 fusion.4
  260.7 4.9 fusion.10
  265.6 4.4 convolution_convert_fusion
  295.8 5.8 collective-permute-done.28
  310.1 18.2 %all_gather.37 = bf16[256,1600]{1,0:T(8,128)(2,1)S(1)} all-gather(bf16[64,1600]{1,0:T(8,128)(2,1)S(1)} %get-tuple-element.298), channel_id=1, replica_groups=mesh['seq'=8,'tp'=4] {'tp'}, dimensions={0}, use_global_device_ids=true | all-gather | bytes 1024000 | tf_op jit(solution)/shard_map/all_gather | solution.py:716
  337.6 4.3 all-to-all-start.1
  352.0 12.4 %all-gather.1 = f32[192,800]{1,0:T(8,128)} all-gather(f32[24,800]{1,0:T(8,128)S(1)} %shard_map.410), channel_id=3, replica_groups=mesh['seq'=8,'tp'=4] {'seq'}, dimensions={0}, use_global_device_ids=true | all-gather | bytes 691200 | tf_op jit(solution)/shard_map/all_gather | solution.py:931
  364.3 4.2 fusion.19
  377.2 4.3 all-to-all-start.2
  394.2 13.3 %shard_map.412 = (bf16[5,320,64]{2,1,0:T(8,128)(2,1)S(1)}, bf16[4,160,1280]{2,1,0:T(8,128)(2,1)}) custom-call(bf16[4,256,160]{2,1,0:T(8,128)(2,1)} %collective-permute-done.7.refs_0_, bf16[4,256,160]{2,1,0:T(8,128)(2,1)} %collective-permute-done.11.refs_1_, bf16[4,256,160]{2,1,0:T(8,128)(2,1)} %collective-permute-done.12.refs_2_, ...), custom_call_target="tpu_custom_call" | custom-call | flops 1048576000 | bytes 8192000 | tf_op jit(solution)/shard_map/pallas_call | solution.py:464
  412.7 19.1 %shard_map.411 = (f32[256,800]{1,0:T(8,128)S(1)}, f32[256,800]{1,0:T(8,128)S(1)}, f32[16,256]{1,0:T(8,128)S(1)}, f32[16,256]{1,0:T(8,128)S(1)}, f32[16,800]{1,0:T(8,128)S(1)}) custom-call(s32[1]{0:T(128)} %bitcast.6.place_ref, f32[8,24,800]{2,1,0:T(8,128)S(1)} %bitcast.215, f32[256,800]{1,0:T(8,128)S(1)} %copy-done.16, f32[256,800]{1,0:T(8,128)S(1)} %copy-done.12, ...), custom_call_target="tpu_custom_call" | custom-call | flops 39321600 | bytes 9011200 | tf_op jit(solution)/shard_map/pallas_call | solution.py:251
  457.7 4.2 all-to-all-done.3
  486.3 8.4 %collective-permute-done.42 = bf16[160,256]{1,0:T(8,128)(2,1)S(1)} collective-permute-done((bf16[160,256]{1,0:T(8,128)(2,1)S(1)}, bf16[160,256]{1,0:T(8,128)(2,1)S(1)}, u32[]{:S(2)}, u32[]{:S(2)}) %collective-permute-start.42) | collective-permute-done | bytes 81952 | tf_op jit(solution)/shard_map/ppermute | solution.py:488
  553.3 7.6 %collective-permute-done.57 = bf16[272,800]{1,0:T(8,128)(2,1)S(1)} collective-permute-done((bf16[272,800]{1,0:T(8,128)(2,1)S(1)}, bf16[272,800]{1,0:T(8,128)(2,1)S(1)}, u32[]{:S(2)}, u32[]{:S(2)}) %collective-permute-start.57) | collective-permute-done | bytes 435232 | tf_op jit(solution)/shard_map/ppermute | solution.py:497
  562.6 5.7 collective-permute-done.60
  569.3 4.4 convert_bitcast_fusion
  (697 shorter events, 302.6 us)
Async XLA Ops:
  7.2 36.6 %all-gather.6.cloned.1.call-start = ((), (), s32[]{:S(2)}) async-start(), calls=%async_computation.6 | async-start | bytes 3225600 | tf_op jit(solution)/shard_map/all_gather | solution.py:739
  8.0 87.6 %all-gather.8.cloned.1.call-start = ((), (), s32[]{:S(2)}) async-start(), calls=%async_computation.7 | async-start | bytes 6451200 | tf_op jit(solution)/shard_map/all_gather | solution.py:739
  10.1 198.3 %all-gather.10.cloned.1.call-start = ((), (), s32[]{:S(2)}) async-start(), calls=%async_computation.8 | async-start | bytes 9216000 | tf_op jit(solution)/shard_map/all_gather | solution.py:742
  88.7 45.6 %collective-permute-start.8 = (bf16[64,1664]{1,0:T(8,128)(2,1)}, bf16[64,1664]{1,0:T(8,128)(2,1)}, u32[]{:S(2)}, u32[]{:S(2)}) collective-permute-start(bf16[64,1664]{1,0:T(8,128)(2,1)} %get-tuple-element.315), channel_id=1, source_target_pairs={{0,1},{1,2},{2,3},{3,0},{4,5},{5,6},{6,7},{7,4},{8,9},{9,10},{10,1... | collective-permute-start | bytes 638984 | tf_op jit(solution)/shard_map/ppermute | solution.py:637
  88.7 43.5 %collective-permute-start.9 = (bf16[64,1664]{1,0:T(8,128)(2,1)}, bf16[64,1664]{1,0:T(8,128)(2,1)}, u32[]{:S(2)}, u32[]{:S(2)}) collective-permute-start(bf16[64,1664]{1,0:T(8,128)(2,1)} %get-tuple-element.315), channel_id=1, source_target_pairs={{0,2},{1,3},{2,0},{3,1},{4,6},{5,7},{6,4},{7,5},{8,10},{9,11},{10,... | collective-permute-start | bytes 638984 | tf_op jit(solution)/shard_map/ppermute | solution.py:637
  91.4 37.9 %collective-permute-start.10 = (bf16[64,1664]{1,0:T(8,128)(2,1)}, bf16[64,1664]{1,0:T(8,128)(2,1)}, u32[]{:S(2)}, u32[]{:S(2)}) collective-permute-start(bf16[64,1664]{1,0:T(8,128)(2,1)} %get-tuple-element.315), channel_id=1, source_target_pairs={{0,3},{1,0},{2,1},{3,2},{4,7},{5,4},{6,5},{7,6},{8,11},{9,8},{10,9... | collective-permute-start | bytes 638984 | tf_op jit(solution)/shard_map/ppermute | solution.py:637
  116.9 43.2 %collective-permute-start.13 = (bf16[4,256,160]{2,1,0:T(8,128)(2,1)S(1)}, bf16[4,256,160]{2,1,0:T(8,128)(2,1)S(1)}, u32[]{:S(2)}, u32[]{:S(2)}) collective-permute-start(bf16[4,256,160]{2,1,0:T(8,128)(2,1)S(1)} %pad_maximum_fusion.14.refs_4_), channel_id=1, source_target_pairs={{0,4},{4,8},{8,12},{12,16},{16,20},{20,24},{24,28},{1,5},{5,9},{9,... | collective-permute-start | bytes 983048 | tf_op jit(solution)/shard_map/ppermute | solution.py:488
  119.2 43.1 %collective-permute-start.12 = (bf16[4,256,160]{2,1,0:T(8,128)(2,1)S(1)}, bf16[4,256,160]{2,1,0:T(8,128)(2,1)}, u32[]{:S(2)}, u32[]{:S(2)}) collective-permute-start(bf16[4,256,160]{2,1,0:T(8,128)(2,1)S(1)} %pad_maximum_fusion.14.refs_4_), channel_id=1, source_target_pairs={{0,8},{4,12},{8,16},{12,20},{16,24},{20,28},{1,9},{5,13},{9,17},{1... | collective-permute-start | bytes 983048 | tf_op jit(solution)/shard_map/ppermute | solution.py:488
  125.2 38.1 %all-to-all-start = ((bf16[4,64,400]{2,1,0:T(8,128)(2,1)}), bf16[4,64,400]{2,1,0:T(8,128)(2,1)}, u32[]{:S(2)}, u32[]{:S(2)}) async-start(bf16[4,64,400]{2,1,0:T(8,128)(2,1)} %bitcast.250), calls=%async_computation | async-start | bytes 524288 | tf_op jit(solution)/shard_map/all_to_all | solution.py:629
  129.2 279.0 %reduce-scatter.3.cloned.1.call-start = ((), (), s32[]{:S(2)}) async-start(), calls=%async_computation.9 | async-start | bytes 6144000 | tf_op jit(solution)/shard_map/reduce_scatter | solution.py:747
  129.3 35.5 %collective-permute-start.11 = (bf16[4,256,160]{2,1,0:T(8,128)(2,1)S(1)}, bf16[4,256,160]{2,1,0:T(8,128)(2,1)}, u32[]{:S(2)}, u32[]{:S(2)}) collective-permute-start(bf16[4,256,160]{2,1,0:T(8,128)(2,1)S(1)} %pad_maximum_fusion.14.refs_4_), channel_id=1, source_target_pairs={{0,12},{4,16},{8,20},{12,24},{16,28},{1,13},{5,17},{9,21},{13,25},... | collective-permute-start | bytes 983048 | tf_op jit(solution)/shard_map/ppermute | solution.py:488
  132.2 37.7 %collective-permute-start.7 = (bf16[4,256,160]{2,1,0:T(8,128)(2,1)S(1)}, bf16[4,256,160]{2,1,0:T(8,128)(2,1)}, u32[]{:S(2)}, u32[]{:S(2)}) collective-permute-start(bf16[4,256,160]{2,1,0:T(8,128)(2,1)S(1)} %pad_maximum_fusion.14.refs_4_), channel_id=1, source_target_pairs={{0,16},{4,20},{8,24},{12,28},{1,17},{5,21},{9,25},{13,29},{2,18},{... | collective-permute-start | bytes 983048 | tf_op jit(solution)/shard_map/ppermute | solution.py:488
  158.5 24.3 %collective-permute-start.17 = (bf16[64,1600]{1,0:T(8,128)(2,1)}, bf16[64,1600]{1,0:T(8,128)(2,1)S(1)}, u32[]{:S(2)}, u32[]{:S(2)}) collective-permute-start(bf16[64,1600]{1,0:T(8,128)(2,1)} %get-tuple-element.278), channel_id=1, source_target_pairs={{0,1},{1,2},{2,3},{3,0},{4,5},{5,6},{6,7},{7,4},{8,9},{9,10},{10,1... | collective-permute-start | bytes 614408 | tf_op jit(solution)/shard_map/ppermute | solution.py:609
  160.1 24.6 %collective-permute-start.19 = (bf16[64,1600]{1,0:T(8,128)(2,1)}, bf16[64,1600]{1,0:T(8,128)(2,1)}, u32[]{:S(2)}, u32[]{:S(2)}) collective-permute-start(bf16[64,1600]{1,0:T(8,128)(2,1)} %get-tuple-element.279), channel_id=1, source_target_pairs={{0,3},{1,0},{2,1},{3,2},{4,7},{5,4},{6,5},{7,6},{8,11},{9,8},{10,9... | collective-permute-start | bytes 614408 | tf_op jit(solution)/shard_map/ppermute | solution.py:609
  162.3 24.4 %collective-permute-start.18 = (bf16[64,1600]{1,0:T(8,128)(2,1)}, bf16[64,1600]{1,0:T(8,128)(2,1)}, u32[]{:S(2)}, u32[]{:S(2)}) collective-permute-start(bf16[64,1600]{1,0:T(8,128)(2,1)} %get-tuple-element.280), channel_id=1, source_target_pairs={{0,2},{1,3},{2,0},{3,1},{4,6},{5,7},{6,4},{7,5},{8,10},{9,11},{10,... | collective-permute-start | bytes 614408 | tf_op jit(solution)/shard_map/ppermute | solution.py:609
  164.7 43.9 %collective-permute-start.23 = (bf16[256,1664]{1,0:T(8,128)(2,1)}, bf16[256,1664]{1,0:T(8,128)(2,1)}, u32[]{:S(2)}, u32[]{:S(2)}) collective-permute-start(bf16[256,1664]{1,0:T(8,128)(2,1)} %bitcast.255), channel_id=1, source_target_pairs={{0,4},{4,0},{8,12},{12,8},{16,20},{20,16},{24,28},{28,24},{1,5},{5... | collective-permute-start | bytes 2555912 | tf_op jit(solution)/shard_map/ppermute | solution.py:497
  292.8 77.8 %collective-permute-start.37 = (bf16[2,400,768]{2,1,0:T(8,128)(2,1)}, bf16[2,400,768]{2,1,0:T(8,128)(2,1)}, u32[]{:S(2)}, u32[]{:S(2)}) collective-permute-start(bf16[2,400,768]{2,1,0:T(8,128)(2,1)} %dynamic-slice_bitcast_fusion), channel_id=1, source_target_pairs={{0,16},{4,20},{8,24},{12,28},{16,0},{20,4},{24,8},{28,12},{1,17},{... | collective-permute-start | bytes 3686408 | tf_op jit(solution)/shard_map/ppermute | solution.py:497
  334.3 105.5 %collective-permute-start.34 = (bf16[64,1600]{1,0:T(8,128)(2,1)}, bf16[64,1600]{1,0:T(8,128)(2,1)}, u32[]{:S(2)}, u32[]{:S(2)}) collective-permute-start(bf16[64,1600]{1,0:T(8,128)(2,1)} %get-tuple-element.269), channel_id=1, source_target_pairs={{0,3},{1,0},{2,1},{3,2},{4,7},{5,4},{6,5},{7,6},{8,11},{9,8},{10,9... | collective-permute-start | bytes 614408 | tf_op jit(solution)/shard_map/ppermute | solution.py:609
  336.6 100.7 %collective-permute-start.33 = (bf16[64,1600]{1,0:T(8,128)(2,1)}, bf16[64,1600]{1,0:T(8,128)(2,1)}, u32[]{:S(2)}, u32[]{:S(2)}) collective-permute-start(bf16[64,1600]{1,0:T(8,128)(2,1)} %get-tuple-element.270), channel_id=1, source_target_pairs={{0,2},{1,3},{2,0},{3,1},{4,6},{5,7},{6,4},{7,5},{8,10},{9,11},{10,... | collective-permute-start | bytes 614408 | tf_op jit(solution)/shard_map/ppermute | solution.py:609
  337.6 37.0 %all-to-all-start.1 = ((bf16[4,64,1600]{2,1,0:T(8,128)(2,1)}), bf16[4,64,1600]{2,1,0:T(8,128)(2,1)}, u32[]{:S(2)}, u32[]{:S(2)}) async-start(bf16[4,64,1600]{2,1,0:T(8,128)(2,1)} %broadcast_in_dim.28), calls=%async_computation.1 | async-start | bytes 1703936 | tf_op jit(solution)/shard_map/all_to_all | solution.py:629
  344.4 94.5 %collective-permute-start.32 = (bf16[64,1600]{1,0:T(8,128)(2,1)}, bf16[64,1600]{1,0:T(8,128)(2,1)}, u32[]{:S(2)}, u32[]{:S(2)}) collective-permute-start(bf16[64,1600]{1,0:T(8,128)(2,1)} %get-tuple-element.271), channel_id=1, source_target_pairs={{0,1},{1,2},{2,3},{3,0},{4,5},{5,6},{6,7},{7,4},{8,9},{9,10},{10,1... | collective-permute-start | bytes 614408 | tf_op jit(solution)/shard_map/ppermute | solution.py:609
  348.1 36.4 %collective-permute-start.31 = (bf16[800,800]{1,0:T(8,128)(2,1)}, bf16[800,800]{1,0:T(8,128)(2,1)}, u32[]{:S(2)}, u32[]{:S(2)}) collective-permute-start(bf16[800,800]{1,0:T(8,128)(2,1)} %convolution_convert_fusion.7), channel_id=1, source_target_pairs={{0,4},{4,0},{8,12},{12,8},{16,20},{20,16},{24,28},{28,24},{1,5},{5... | collective-permute-start | bytes 3840008 | tf_op jit(solution)/shard_map/ppermute | solution.py:497
  381.5 88.9 %reduce-scatter.5.cloned.1.call-start = ((), (), s32[]{:S(2)}) async-start(), calls=%async_computation.10 | async-start | bytes 2048000 | tf_op jit(solution)/shard_map/reduce_scatter | solution.py:945
  384.4 96.2 %collective-permute-start.47 = (bf16[400,768]{1,0:T(8,128)(2,1)}, bf16[400,768]{1,0:T(8,128)(2,1)}, u32[]{:S(2)}, u32[]{:S(2)}) collective-permute-start(bf16[400,768]{1,0:T(8,128)(2,1)} %dynamic-slice_bitcast_fusion.6), channel_id=1, source_target_pairs={{0,8},{4,12},{8,0},{12,4},{16,24},{20,28},{24,16},{28,20},{1,9},{5... | collective-permute-start | bytes 1843208 | tf_op jit(solution)/shard_map/ppermute | solution.py:497
  389.6 80.8 %collective-permute-start.40 = (bf16[2,200,800]{2,1,0:T(8,128)(2,1)}, bf16[2,200,800]{2,1,0:T(8,128)(2,1)}, u32[]{:S(2)}, u32[]{:S(2)}) collective-permute-start(bf16[2,200,800]{2,1,0:T(8,128)(2,1)} %dynamic-slice_bitcast_fusion.2), channel_id=1, source_target_pairs={{0,8},{4,12},{8,0},{12,4},{16,24},{20,28},{24,16},{28,20},{1,9},{5... | collective-permute-start | bytes 1920008 | tf_op jit(solution)/shard_map/ppermute | solution.py:497
  438.9 37.8 %collective-permute-start.39 = (bf16[2,200,800]{2,1,0:T(8,128)(2,1)}, bf16[2,200,800]{2,1,0:T(8,128)(2,1)}, u32[]{:S(2)}, u32[]{:S(2)}) collective-permute-start(bf16[2,200,800]{2,1,0:T(8,128)(2,1)} %dynamic-slice_bitcast_fusion.3), channel_id=1, source_target_pairs={{0,16},{4,20},{8,24},{12,28},{16,0},{20,4},{24,8},{28,12},{1,17},{... | collective-permute-start | bytes 1920008 | tf_op jit(solution)/shard_map/ppermute | solution.py:497
  454.0 115.3 %all-reduce.25.cloned.1.call-start = ((), (), s32[]{:S(2)}) async-start(), calls=%async_computation.11 | async-start | bytes 5324800 | tf_op jit(solution)/shard_map/psum | solution.py:951
  470.2 50.9 %collective-permute-start.45 = (bf16[200,1536]{1,0:T(8,128)(2,1)}, bf16[200,1536]{1,0:T(8,128)(2,1)}, u32[]{:S(2)}, u32[]{:S(2)}) collective-permute-start(bf16[200,1536]{1,0:T(8,128)(2,1)} %dynamic-slice_bitcast_fusion.5), channel_id=1, source_target_pairs={{0,4},{4,0},{8,12},{12,8},{16,20},{20,16},{24,28},{28,24},{1,5},{5... | collective-permute-start | bytes 1843208 | tf_op jit(solution)/shard_map/ppermute | solution.py:497
  494.7 19.4 %collective-permute-start.50 = (bf16[200,800]{1,0:T(8,128)(2,1)}, bf16[200,800]{1,0:T(8,128)(2,1)}, u32[]{:S(2)}, u32[]{:S(2)}) collective-permute-start(bf16[200,800]{1,0:T(8,128)(2,1)} %dynamic-slice_bitcast_fusion.8), channel_id=1, source_target_pairs={{0,16},{4,20},{8,24},{12,28},{16,0},{20,4},{24,8},{28,12},{1,17},{... | collective-permute-start | bytes 960008 | tf_op jit(solution)/shard_map/ppermute | solution.py:497
  497.3 20.9 %collective-permute-start.49 = (bf16[200,800]{1,0:T(8,128)(2,1)}, bf16[200,800]{1,0:T(8,128)(2,1)}, u32[]{:S(2)}, u32[]{:S(2)}) collective-permute-start(bf16[200,800]{1,0:T(8,128)(2,1)} %dynamic-slice_bitcast_fusion.9), channel_id=1, source_target_pairs={{0,8},{4,12},{8,0},{12,4},{16,24},{20,28},{24,16},{28,20},{1,9},{5... | collective-permute-start | bytes 960008 | tf_op jit(solution)/shard_map/ppermute | solution.py:497
  518.5 30.5 %collective-permute-start.59 = (bf16[2,200,800]{2,1,0:T(8,128)(2,1)}, bf16[2,200,800]{2,1,0:T(8,128)(2,1)}, u32[]{:S(2)}, u32[]{:S(2)}) collective-permute-start(bf16[2,200,800]{2,1,0:T(8,128)(2,1)} %dynamic-slice_bitcast_fusion.1), channel_id=1, source_target_pairs={{0,16},{4,20},{8,24},{12,28},{16,0},{20,4},{24,8},{28,12},{1,17},{... | collective-permute-start | bytes 1920008 | tf_op jit(solution)/shard_map/ppermute | solution.py:497
  551.9 21.9 %collective-permute-start.63 = (bf16[160,1600]{1,0:T(8,128)(2,1)S(1)}, bf16[160,1600]{1,0:T(8,128)(2,1)S(1)}, u32[]{:S(2)}, u32[]{:S(2)}) collective-permute-start(bf16[160,1600]{1,0:T(8,128)(2,1)S(1)} %add_convert_fusion.3), channel_id=1, source_target_pairs={{0,16},{4,20},{8,24},{12,28},{16,0},{20,4},{24,8},{28,12},{1,17},{... | collective-permute-start | bytes 1536008 | tf_op jit(solution)/shard_map/ppermute | solution.py:497
  (219 other events, 2205.4 us)
Sparse Core Ops, SparseCore 0:
  9.9 33.8 all-gather.5
  46.3 43.2 all-gather.7
  92.0 111.8 all-gather.9
  270.2 82.4 reduce-scatter.2
  408.4 37.5 reduce-scatter.4
  465.6 73.6 all-reduce.24
